TPU v7x, 256 devices: a whole 4x4x8 slice. The times are simulated.
256 devices in a mesh: dom: 8 (over x_hi, y), slab: 32 (over z, x_lo, core).
Axes of the slice: x: 4 (x_hi: 2, x_lo: 2; x = x_hi * 2 + x_lo), y: 4, z: 8, core: 2. Of those that a mesh axis runs over, the one named last changes fastest.
Arguments:
- images: bfloat16 [2048, 256, 512], P(('dom', 'slab')), may hold values from -6 to 6
- orient_ids: int32 [2048], P(('dom', 'slab')), may hold values from 0 to 5
- shift_ids: int32 [2048], P(('dom', 'slab')), may hold values from 0 to 15
- group_ids: int32 [2048], P(('dom', 'slab')), may hold values from 0 to 7
- translations: float32 [16, 2], replicated, may hold values from -6 to 6
- defocus: float32 [8], replicated, may hold values from 2 to 24
- in_plane: bfloat16 [6, 256, 256], replicated, may hold values from -0.375 to 0.375
- slab_rows: bfloat16 [6, 256, 256, 256], P(None, 'slab'), may hold values from -0.15625 to 0.15625
Outputs:
- density: float32 [256, 256, 256], P('slab', 'dom')
All inputs are finite; a program needn't handle non-finite values.
Results may differ from a plain program's by a relative error of at most 0.007.
Values may be sent and summed in bfloat16 or wider, within the bound.
No kernel may reach another device: no remote copies, remote signals or barrier semaphores. Data moves between devices by JAX's collectives and lax.ppermute only.
A program may use at most 64 MiB of HBM per device.

v0:
```python
import math

import jax
import jax.numpy as jnp
from jax import lax
from jax.sharding import PartitionSpec as P

ORIENT = 6


def frequencies(length):
    position = jnp.arange(length, dtype=jnp.int32)
    return jnp.where(position < length // 2, position, position - length).astype(jnp.float32)


def dft_tables(length):
    position = jnp.arange(length, dtype=jnp.int32)
    product = position[:, None] * position[None, :] % length
    angles = product.astype(jnp.float32) * (2.0 * math.pi / length)
    return (jnp.cos(angles), jnp.sin(angles))


def weight_images(images, shifts, focus_values):
    length = images.shape[1]
    frequency = frequencies(length)
    radius = (frequency[:, None] ** 2 + frequency[None, :] ** 2) / float((length // 2) ** 2)
    phase_angle = (
        2.0
        * math.pi
        / length
        * (
            shifts[:, 0, None, None] * frequency[None, :, None]
            + shifts[:, 1, None, None] * frequency[None, None, :]
        )
    )
    contrast = -jnp.sin(focus_values[:, None, None] * radius[None] + 0.1)
    real_part = images[:, :, :length].astype(jnp.float32)
    imag_part = images[:, :, length:].astype(jnp.float32)
    cosine = jnp.cos(phase_angle)
    sine_table = jnp.sin(phase_angle)
    return jnp.concatenate(
        [
            contrast * (real_part * cosine + imag_part * sine_table),
            contrast * (imag_part * cosine - real_part * sine_table),
        ],
        axis=2,
    )


def mix_columns(class_total, in_plane):
    classes, row_count, columns = class_total.shape
    halves = class_total.reshape(classes, row_count, 2, columns // 2)
    product = jnp.einsum("okrx,oxw->okrw", halves, in_plane, preferred_element_type=jnp.float32)
    return product.astype(jnp.bfloat16).reshape(classes, row_count, columns)


def along_x(planes, block_matrix):
    flat = planes.reshape(-1, planes.shape[-1])
    result = jnp.dot(
        flat, block_matrix, precision=lax.Precision.HIGHEST, preferred_element_type=jnp.float32
    )
    return result.reshape(planes.shape)


def along_y(planes, cosine_rows, sine_rows):
    length = planes.shape[-1] // 2
    with_cosine = jnp.einsum("yk,zkc->zyc", cosine_rows, planes, precision=lax.Precision.HIGHEST)
    with_sine = jnp.einsum("yk,zkc->zyc", sine_rows, planes, precision=lax.Precision.HIGHEST)
    real_part = with_cosine[:, :, :length] - with_sine[:, :, length:]
    imag_part = with_sine[:, :, :length] + with_cosine[:, :, length:]
    return jnp.concatenate([real_part, imag_part], axis=2)


def on_device(images, orient_ids, shift_ids, group_ids, translations, defocus, in_plane, slab_rows):
    length = images.shape[1]
    own_images = images.shape[0]
    trans_hot = (
        shift_ids[:, None] == jnp.arange(translations.shape[0], dtype=jnp.int32)[None, :]
    ).astype(jnp.float32)
    shifts = jnp.dot(
        trans_hot, translations, precision=lax.Precision.HIGHEST, preferred_element_type=jnp.float32
    )
    focus_hot = (
        group_ids[:, None] == jnp.arange(defocus.shape[0], dtype=jnp.int32)[None, :]
    ).astype(jnp.float32)
    focus_values = jnp.sum(focus_hot * defocus[None, :], axis=1)
    weighted = weight_images(images, shifts, focus_values)
    class_hot = (orient_ids[None, :] == jnp.arange(ORIENT, dtype=jnp.int32)[:, None]).astype(
        jnp.float32
    )
    local_sums = jnp.dot(
        class_hot,
        weighted.reshape(own_images, -1),
        precision=lax.Precision.HIGHEST,
        preferred_element_type=jnp.float32,
    ).reshape(ORIENT, length, 2 * length)
    summed = lax.psum(local_sums, "slab")
    mixed_rows = mix_columns(summed.astype(jnp.bfloat16), in_plane)
    cosine_table, sine_table = dft_tables(length)
    block_matrix = jnp.concatenate(
        [
            jnp.concatenate([cosine_table, sine_table], axis=1),
            jnp.concatenate([-sine_table, cosine_table], axis=1),
        ],
        axis=0,
    )
    dom_count = lax.axis_size("dom")
    own_y = length // dom_count
    plane_count = slab_rows.shape[1]
    volume = jnp.einsum("ozyk,okc->zyc", slab_rows, mixed_rows, preferred_element_type=jnp.float32)
    planes = along_y(along_x(volume, block_matrix), cosine_table, sine_table)
    row_planes = lax.psum_scatter(planes, "dom", scatter_dimension=1, tiled=True)
    slab_count = lax.axis_size("slab")
    own_x = length // slab_count
    blocks = row_planes.reshape(plane_count, own_y, 2, slab_count, own_x)
    pencil = lax.all_to_all(blocks, "slab", split_axis=3, concat_axis=0, tiled=True)
    real_part = pencil[:, :, 0, 0, :]
    imag_part = pencil[:, :, 1, 0, :]
    result = jnp.einsum(
        "kz,kyx->xyz", cosine_table, real_part, precision=lax.Precision.HIGHEST
    ) - jnp.einsum("kz,kyx->xyz", sine_table, imag_part, precision=lax.Precision.HIGHEST)
    total_parts = own_images * dom_count * slab_count
    scaling = 1.0 / (length**1.5 * math.sqrt(total_parts))
    return result * scaling


def solution(mesh):
    return jax.shard_map(
        on_device,
        mesh=mesh,
        in_specs=(
            P(("dom", "slab"), None, None),
            P(("dom", "slab")),
            P(("dom", "slab")),
            P(("dom", "slab")),
            P(),
            P(),
            P(),
            P(None, "slab", None, None),
        ),
        out_specs=P("slab", "dom", None),
        check_vma=False,
    )
```

profile of v0, /device:TPU:1, one launch (start us, length us, event | category | flops | bytes accessed | tf_op | source)
XLA Modules:
  0.0 342.3 jit_solution(5080919842518080571)
XLA Ops:
  6.6 1.0 fusion.30
  7.6 1.0 fusion.34
  8.6 0.9 fusion.40
  9.6 0.9 select_reduce_fusion
  10.5 17.0 %fusion.3 = (f32[8,256,256]{2,1,0:T(8,128)S(1)}, f32[8,256,256]{2,1,0:T(8,128)S(1)}) fusion(f32[8,256]{1,0:T(8,128)S(1)} %get-tuple-element.12, f32[8,256]{1,0:T(8,128)S(1)} %get-tuple-element.11, f32[256,256]{1,0:T(8,128)S(1)} %add_multiply_fusion.1, f32[8]{0:T(128)S(1)} %select_reduce_fusion, bf16[8,256,512]{2,1,0:T(8,128)(2,1)} %param.8), kind=kLoop, calls=%fused_computation.11 | loop fusion | flops 7864320 | bytes 6570016 | tf_op jit(solution)/shard_map/mul | solution.py:43
  27.5 0.6 maximum_bitcast_fusion
  28.2 4.5 %fusion.38 = f32[6,256,512]{2,0,1:T(8,128)S(1)} fusion(s32[8]{0:T(128)S(1)} %copy-done.3, f32[1,8,256,512]{3,2,1,0:T(8,128)S(1)} %maximum_bitcast_fusion), kind=kOutput, calls=%fused_computation.59 | convolution fusion | flops 75497520 | bytes 7340064 | tf_op jit(solution)/shard_map/dot_general | solution.py:91
  32.7 3.5 %copy.75 = f32[6,256,512]{2,1,0:T(8,128)} copy(f32[6,256,512]{2,0,1:T(8,128)S(1)} %fusion.38) | data formatting | bytes 6291456 | tf_op jit(solution)/shard_map/dot_general | solution.py:91
  36.2 132.9 %all-reduce.1 = bf16[6,256,512]{2,1,0:T(8,128)(2,1)S(1)} all-reduce(f32[6,256,512]{2,1,0:T(8,128)} %copy.75), channel_id=1, replica_groups=mesh['dom'=8,'slab'=32] {'slab'}, use_global_device_ids=true, to_apply=%region_1.2 | all-reduce | flops 786432 | bytes 4718592 | tf_op jit(solution)/shard_map/psum | solution.py:97
  169.1 1.6 copy.76
  170.6 2.0 convolution_convert_fusion
  172.7 5.7 %fusion.65 = f32[512,8,256,1]{2,0,1,3:T(8,128)S(1)} fusion(bf16[6,256,512,1]{1,2,3,0:T(8,128)(2,1)S(1)} %bitcast.80, bf16[6,8,256,256]{3,2,1,0:T(8,128)(2,1)} %param.15), kind=kOutput, calls=%fused_computation.89 | convolution fusion | flops 3221225472 | bytes 12058624 | tf_op jit(solution)/shard_map/ozyk,okc->zyc/dot_general | solution.py:110
  178.4 7.6 %fusion = f32[8,256,512]{1,2,0:T(8,128)S(1)} fusion(f32[512,8,256,1]{2,0,1,3:T(8,128)S(1)} %fusion.65, f32[256,256]{1,0:T(8,128)S(1)} %get-tuple-element.16, f32[256,256]{1,0:T(8,128)S(1)} %fusion.34, f32[256,256]{1,0:T(8,128)S(1)} %get-tuple-element.15), kind=kOutput, calls=%fused_computation | convolution fusion | flops 6443237376 | bytes 9175040 | tf_op jit(solution)/shard_map/dot_general | solution.py:59
  186.0 4.6 %convolution_bitcast_fusion = f32[8,256,512]{1,2,0:T(8,128)S(1)} fusion(f32[8,256,512]{1,2,0:T(8,128)S(1)} %fusion), kind=kOutput, calls=%fused_computation.8 | convolution fusion | flops 3222142976 | bytes 8388608 | tf_op jit(solution)/shard_map/yk,zkc->zyc/dot_general | solution.py:68
  190.6 4.8 %convolution_bitcast_fusion.1 = f32[8,256,512]{1,2,0:T(8,128)S(1)} fusion(f32[8,256,512]{1,2,0:T(8,128)S(1)} %fusion), kind=kOutput, calls=%fused_computation.9 | convolution fusion | flops 3222142976 | bytes 8388608 | tf_op jit(solution)/shard_map/yk,zkc->zyc/dot_general | solution.py:67
  195.4 0.6 slice_subtract_fusion
  196.1 2.4 pad_maximum_fusion
  198.5 5.6 %copy.83 = f32[8,256,512]{2,0,1:T(8,128)} copy(f32[8,256,512]{1,2,0:T(8,128)} %pad_maximum_fusion) | data formatting | bytes 8388608 | tf_op jit(solution)/shard_map/concatenate | solution.py:71
  204.1 89.5 %reduce-scatter.2.cloned.1.call-done = f32[8,32,512]{2,0,1:T(8,128)} async-done(((f32[8,256,512]{2,0,1:T(8,128)}), f32[8,32,512]{2,0,1:T(8,128)}) %reduce-scatter.2.cloned.1.call-update) | async-done | bytes 524304 | tf_op jit(solution)/shard_map/reduce_scatter | solution.py:112
  293.6 1.7 copy.84
  295.3 1.6 copy.104
  296.9 2.5 reshape.168
  299.4 25.7 %all_to_all.18 = f32[32,1,4096]{2,1,0:T(1,128)S(1)} all-to-all(f32[32,1,4096]{2,1,0:T(1,128)S(1)} %reshape.168), channel_id=1, replica_groups=mesh['dom'=8,'slab'=32] {'slab'}, dimensions={0} | all-to-all | bytes 1048576 | tf_op jit(solution)/shard_map/all_to_all | solution.py:116
  325.0 0.5 broadcast.141
  325.5 1.9 reduce
  327.4 0.7 reshape.169
  328.1 1.5 fusion.62
  329.6 1.7 copy.96
  331.3 1.3 fusion.21
  332.7 0.4 copy.97
  333.1 1.4 fusion.9
  334.4 0.8 copy.88
  (15 shorter events, 0.3 us)
Async XLA Ops:
  6.5 164.1 %copy-start = (bf16[6,256,256]{2,1,0:T(8,128)(2,1)S(1)}, bf16[6,256,256]{2,1,0:T(8,128)(2,1)}, u32[]{:S(2)}) copy-start(bf16[6,256,256]{2,1,0:T(8,128)(2,1)} %param.14) | copy-start | bytes 2359300
  6.5 287.1 %reduce-scatter.2.cloned.1.call-start = ((), (), s32[]{:S(2)}) async-start(), calls=%async_computation.2 | async-start | bytes 4718592 | tf_op jit(solution)/shard_map/reduce_scatter | solution.py:112
  27.5 0.7 copy-start.3
  329.6 3.1 copy-start.2
  329.6 5.6 %copy-start.1 = (bf16[6,256,256]{2,1,0:T(8,128)(2,1)S(1)}, bf16[6,256,256]{2,1,0:T(8,128)(2,1)}, u32[]{:S(2)}) copy-start(bf16[6,256,256]{2,1,0:T(8,128)(2,1)} %param.14) | copy-start | bytes 2359300
Sparse Core Ops, SparseCore 0:
  204.2 89.3 reduce-scatter.1
where the time goes:
time: 345 us; the launch traced here: 342 us
  blocking collectives  159 us (46%)
  waiting for transfers between devices  89.5 us (26%)
  matrix products  32.8 us (10%)
  other arithmetic  25.6 us (7%)
  local copies, waits for them, and re-layouts  22 us (6%)
  between operations  13.8 us (4%)
    psum x1, blocking collectives, on_device(): summed = lax.psum(local_sums, 'slab')  133 us
    reduce_scatter x1, waiting for transfers between devices, on_device(): lax.psum_scatter(planes, 'dom', scatter_dimension=1, tiled=True)  89.5 us
    all_to_all x1, blocking collectives, on_device(): lax.all_to_all(blocks, 'slab', split_axis=3, concat_axis=0, tiled=True)  25.7 us
    mul x1, other arithmetic, weight_images(): contrast * (real_part * cosine + imag_part * sine_table)  17 us
    dot_general x1, matrix products, along_x(): jnp.dot(flat, block_matrix, precision=lax.Precision.HIGHEST, preferred_el...  7.6 us
  transfers between devices with their start and end apart: 1, of which 1 were waited for; matrix products, arithmetic and copies ran while one was open for 0% of the time, Pallas kernels for 0%

commit v1 on v0

v1 whole, which is shorter than its diff:
```python
import math

import jax
import jax.numpy as jnp
import numpy as np
from jax import lax
from jax.experimental import pallas as pl
from jax.experimental.pallas import tpu as pltpu
from jax.sharding import Mesh
from jax.sharding import PartitionSpec as P

N = 256
ORIENT = 6
IMG = 8
BF16 = jnp.bfloat16
F32 = jnp.float32

DOM = ("xh", "yy")
SLAB = ("zz", "xl", "co")
ALL = DOM + SLAB


def split_table(table):
    high = table.astype(jnp.bfloat16)
    low = (table - high.astype(np.float64)).astype(jnp.bfloat16)
    return high, low


def phases(left, right):
    angles = (np.outer(left, right) % N) * (2.0 * math.pi / N)
    return np.cos(angles), np.sin(angles)


def x_table():
    x_of = (8 * np.arange(32)[None, :] + np.arange(8)[:, None]).reshape(-1)
    cosine, sine = (t.reshape(8, 32, N) for t in phases(x_of, np.arange(N)))
    real_rows = np.concatenate([cosine, -sine], axis=2)
    imag_rows = np.concatenate([sine, cosine], axis=2)
    return split_table(np.stack([real_rows, imag_rows], axis=1).reshape(512, 512))


def y_table():
    cosine, sine = (t.reshape(N, 8, 32) for t in phases(np.arange(N), np.arange(N)))
    from_real = np.stack([cosine, sine], axis=2).reshape(N, 512)
    from_imag = np.stack([-sine, cosine], axis=2).reshape(N, 512)
    return split_table(np.concatenate([from_real, from_imag], axis=0))


def z_table():
    half, slab, part = np.meshgrid(np.arange(2), np.arange(32), np.arange(4), indexing="ij")
    kz_of = (8 * slab + 4 * half + part).reshape(-1)
    cosine, sine = (t.reshape(2, 128, N) for t in phases(kz_of, np.arange(N)))
    return split_table(np.stack([cosine, -sine], axis=1).reshape(512, N))


def rows_dot(left, right):
    return lax.dot_general(left, right, (((1,), (1,)), ((), ())), preferred_element_type=F32)


def plain_dot(left, right):
    return jnp.dot(left, right, preferred_element_type=F32)


def front_kernel(
    orient, shift, group, trans, defocus, core, images, in_plane, x_high, x_low, keep, send, total
):
    position = lax.broadcasted_iota(jnp.int32, (IMG, N), 1)
    freq = jnp.where(position < N // 2, position, position - N).astype(F32)
    row = lax.broadcasted_iota(jnp.int32, (IMG, N), 0)
    shift_y = jnp.zeros((IMG, N), F32)
    shift_x = jnp.zeros((IMG, N), F32)
    focus = jnp.zeros((IMG, N), F32)
    for p in range(IMG):
        shift_y = jnp.where(row == p, trans[shift[p], 0], shift_y)
        shift_x = jnp.where(row == p, trans[shift[p], 1], shift_x)
        focus = jnp.where(row == p, defocus[group[p]], focus)
    squares = freq * freq * (1.0 / (N // 2) ** 2)
    step = 2.0 * math.pi / N
    angles = jnp.concatenate(
        [
            step * shift_y * freq,
            focus * squares + 0.1,
            step * shift_x * freq,
            focus * squares,
        ],
        axis=0,
    )
    sines = jnp.sin(angles)
    cosines = jnp.cos(angles)
    columns = jnp.concatenate([sines, cosines, jnp.zeros((64, N), F32)], axis=0).T
    total[...] = jnp.zeros_like(total)
    chunk = 32
    for p in range(IMG):
        sin_tx, sin_fx = sines[16 + p : 17 + p], sines[24 + p : 25 + p]
        cos_tx, cos_fx = cosines[16 + p : 17 + p], cosines[24 + p : 25 + p]
        which = orient[p]
        for r in range(0, N, chunk):
            rows = slice(r, r + chunk)
            sin_ty = columns[rows, p : p + 1]
            sin_fy = columns[rows, 8 + p : 9 + p]
            cos_ty = columns[rows, 32 + p : 33 + p]
            cos_fy = columns[rows, 40 + p : 41 + p]
            contrast = -(sin_fy * cos_fx + cos_fy * sin_fx)
            turn_re = contrast * (cos_ty * cos_tx - sin_ty * sin_tx)
            turn_im = contrast * (sin_ty * cos_tx + cos_ty * sin_tx)
            real_part = images[p, rows, :N].astype(F32)
            imag_part = images[p, rows, N:].astype(F32)
            total[which, rows, :N] += real_part * turn_re + imag_part * turn_im
            total[which, rows, N:] += imag_part * turn_re - real_part * turn_im
    first = core[0] == 0
    for o in range(ORIENT):
        sums = total[o].astype(BF16)
        matrix = in_plane[o]
        mixed = jnp.concatenate(
            [plain_dot(sums[:, :N], matrix), plain_dot(sums[:, N:], matrix)], axis=1
        ).astype(BF16)
        along = rows_dot(x_high[...], mixed) + rows_dot(x_low[...], mixed)
        along = along.astype(BF16)
        low_half, high_half = along[:, :128], along[:, 128:]
        own = jnp.where(first, low_half, high_half)
        other = jnp.where(first, high_half, low_half)
        for d in range(8):
            keep[d, 64 * o : 64 * o + 64, :] = own[64 * d : 64 * d + 64]
            send[d, 64 * o : 64 * o + 64, :] = other[64 * d : 64 * d + 64]


def insert_kernel(gathered, slab_rows, y_high, y_low, out, rows_all, spectrum):
    plane = pl.program_id(0)

    @pl.when(plane == 0)
    def _():
        for i in range(16):
            for c in range(2):
                rows_all[24 * i : 24 * i + 24, 128 * c : 128 * c + 128] = gathered[
                    2 * i + c
                ].astype(F32)

    found = jnp.zeros((64, N), F32)
    for o in range(ORIENT):
        found += rows_dot(rows_all[64 * o : 64 * o + 64, :].astype(BF16), slab_rows[o, 0])
    start = (plane // 4) * 128 + plane % 4
    for part in range(4):
        rows, lanes = 32 * (part // 2), 128 * (part % 2)
        spectrum[part, pl.ds(start, 32, stride=4), :] = found[rows : rows + 32, lanes : lanes + 128]

    @pl.when(plane == pl.num_programs(0) - 1)
    def _():
        lane = lax.broadcasted_iota(jnp.int32, (128, 128), 1)
        both = jnp.concatenate([spectrum[part] for part in range(4)], axis=1).astype(BF16)
        result = plain_dot(both, y_high[...]) + plain_dot(both, y_low[...])
        for e in range(4):
            early = result[:128, 128 * e : 128 * e + 128]
            late = result[128:, 128 * e : 128 * e + 128]
            even = jnp.where(lane < 64, early, pltpu.roll(late, 64, 1))
            odd = jnp.where(lane < 64, pltpu.roll(early, 64, 1), late)
            out[2 * e] = even.astype(BF16)
            out[2 * e + 1] = odd.astype(BF16)


def last_kernel(pencils, z_high, z_low, out):
    scaling = 1.0 / (N**1.5 * math.sqrt(2048))
    rows = []
    for d in range(8):
        turned = pencils[d].astype(F32).T.astype(BF16)
        rows.append(jnp.concatenate([turned[32 * q : 32 * q + 32] for q in range(4)], axis=1))
    stacked = jnp.concatenate(rows, axis=0)
    result = plain_dot(stacked, z_high[...]) + plain_dot(stacked, z_low[...])
    for d in range(8):
        out[d] = result[32 * d : 32 * d + 32] * scaling


VMEM_SPEC = pl.BlockSpec(memory_space=pltpu.VMEM)
SMEM_SPEC = pl.BlockSpec(memory_space=pltpu.SMEM)
LIMIT = 48 * 1024 * 1024


def on_device(images, orient_ids, shift_ids, group_ids, translations, defocus, in_plane, slab_rows):
    core = lax.axis_index("co").astype(jnp.int32).reshape(1)
    x_high, x_low = x_table()
    keep, send = pl.pallas_call(
        front_kernel,
        out_shape=[jax.ShapeDtypeStruct((8, 384, 128), BF16)] * 2,
        in_specs=[SMEM_SPEC] * 6 + [VMEM_SPEC] * 4,
        out_specs=[VMEM_SPEC] * 2,
        scratch_shapes=[pltpu.VMEM((ORIENT, N, 2 * N), F32)],
        compiler_params=pltpu.CompilerParams(vmem_limit_bytes=LIMIT),
        name="front",
    )(
        orient_ids, shift_ids, group_ids, translations, defocus, core,
        images, in_plane, jnp.asarray(x_high), jnp.asarray(x_low),
    )
    other = lax.ppermute(send, "co", [(0, 1), (1, 0)])
    pair = (keep.astype(F32) + other.astype(F32)).astype(BF16)
    pieces = lax.all_to_all(pair, DOM, split_axis=0, concat_axis=0, tiled=True)
    part = jnp.sum(pieces.astype(F32), axis=0).astype(BF16)
    pieces = lax.all_to_all(
        part.reshape(16, 24, 128), ("zz", "xl"), split_axis=0, concat_axis=0, tiled=True
    )
    part = jnp.sum(pieces.astype(F32), axis=0).astype(BF16)
    gathered = lax.all_to_all(
        jnp.broadcast_to(part[None], (32, 24, 128)), SLAB, split_axis=0, concat_axis=0, tiled=True
    )
    y_high, y_low = y_table()
    planes = slab_rows.shape[1]
    sent = pl.pallas_call(
        insert_kernel,
        out_shape=jax.ShapeDtypeStruct((8, 128, 128), BF16),
        grid=(planes,),
        in_specs=[
            pl.BlockSpec((32, 24, 128), lambda i: (0, 0, 0)),
            pl.BlockSpec((ORIENT, 1, N, N), lambda i: (0, i, 0, 0)),
            pl.BlockSpec((512, 512), lambda i: (0, 0)),
            pl.BlockSpec((512, 512), lambda i: (0, 0)),
        ],
        out_specs=pl.BlockSpec((8, 128, 128), lambda i: (0, 0, 0)),
        scratch_shapes=[pltpu.VMEM((384, N), F32), pltpu.VMEM((4, N, 128), F32)],
        compiler_params=pltpu.CompilerParams(vmem_limit_bytes=LIMIT),
        name="insert",
    )(gathered, slab_rows, jnp.asarray(y_high), jnp.asarray(y_low))
    pencils = lax.all_to_all(
        sent.reshape(256, 4, 128), ALL, split_axis=0, concat_axis=0, tiled=True
    )
    z_high, z_low = z_table()
    return pl.pallas_call(
        last_kernel,
        out_shape=jax.ShapeDtypeStruct((8, 32, N), F32),
        in_specs=[VMEM_SPEC] * 3,
        out_specs=VMEM_SPEC,
        compiler_params=pltpu.CompilerParams(vmem_limit_bytes=LIMIT),
        name="last",
    )(pencils.reshape(8, 128, 128), jnp.asarray(z_high), jnp.asarray(z_low))


def solution(mesh):
    fine = Mesh(mesh.devices.reshape(2, 4, 8, 2, 2), ALL)
    return jax.shard_map(
        on_device,
        mesh=fine,
        in_specs=(
            P(ALL, None, None),
            P(ALL),
            P(ALL),
            P(ALL),
            P(),
            P(),
            P(),
            P(None, SLAB, None, None),
        ),
        out_specs=P(SLAB, DOM, None),
        check_vma=False,
    )
```

time: 345 us -> 100 us (0.29)
  waiting for transfers between devices: 89.5 us -> 1.91 us
  blocking collectives: 159 us -> 72.3 us
  matrix products: 32.8 us -> 0 us
  other arithmetic: 25.6 us -> 0.34 us
  local copies, waits for them, and re-layouts: 22 us -> 8.23 us
  between operations: 13.8 us -> 0.07 us
  Pallas kernels: 0 us -> 13.6 us
    psum x1 -> x0, blocking collectives: 133 us -> none  [on_device(): summed = lax.psum(local_sums, 'slab')]
    reduce_scatter x1 -> x0, waiting for transfers between devices: 89.5 us -> none  [on_device(): lax.psum_scatter(planes, 'dom', scatter_dimension=1, tiled=True)]
    all_to_all x1 -> x4, blocking collectives: 25.7 us -> 72.3 us  [the longest x1 21.4 us: on_device(): lax.all_to_all(sent.reshape(256, 4, 128), ALL, split_axis=0, concat_axis=...]
    dot_general x9 -> x0, matrix products: 32.8 us -> none  [the longest x1 7.6 us: along_x(): jnp.dot(flat, block_matrix, precision=lax.Precision.HIGHEST, preferred_el...]
    mul x2 -> x0, other arithmetic: 17.1 us -> none  [the longest x1 17 us: weight_images(): contrast * (real_part * cosine + imag_part * sine_table)]
    pallas_call x0 -> x3, Pallas kernels: none -> 13.6 us  [the longest x1 7.18 us: on_device(): pl.pallas_call(insert_kernel, out_shape=jax.ShapeDtypeStruct((8, 128, 128...]
    concatenate x1 -> x0, local copies, waits for them, and re-layouts: 5.57 us -> none  [along_y(): return jnp.concatenate([real_part, imag_part], axis=2)]
    dot_general x1 -> x0, local copies, waits for them, and re-layouts: 3.48 us -> none  [on_device(): jnp.dot(class_hot, weighted.reshape(own_images, -1), precision=lax.Precis...]
where the time goes in v1:
time: 100 us; the launch traced here: 99.8 us
  blocking collectives  72.3 us (72%)
  Pallas kernels  13.6 us (14%)
  local copies, waits for them, and re-layouts  8.23 us (8%)
  starting transfers between devices  3.33 us (3%)
  waiting for transfers between devices  1.91 us (2%)
    all_to_all x1, blocking collectives, on_device(): lax.all_to_all(sent.reshape(256, 4, 128), ALL, split_axis=0, concat_axis=...  21.4 us
    all_to_all x1, blocking collectives, on_device(): pieces = lax.all_to_all(pair, DOM, split_axis=0, concat_axis=0, tiled=True)  17.7 us
    all_to_all x1, blocking collectives, on_device(): lax.all_to_all(jnp.broadcast_to(part[None], (32, 24, 128)), SLAB, split_a...  16.8 us
    all_to_all x1, blocking collectives, on_device(): lax.all_to_all(part.reshape(16, 24, 128), ('zz', 'xl'), split_axis=0, con...  16.4 us
    unnamed x25, local copies, waits for them, and re-layouts  8.2 us
    pallas_call x1, Pallas kernels, on_device(): pl.pallas_call(insert_kernel, out_shape=jax.ShapeDtypeStruct((8, 128, 128...  7.18 us
    pallas_call x1, Pallas kernels, on_device(): pl.pallas_call(front_kernel, out_shape=[jax.ShapeDtypeStruct((8, 384, 128...  5.38 us
    ppermute x1, starting transfers between devices, on_device(): other = lax.ppermute(send, 'co', [(0, 1), (1, 0)])  3.33 us
  transfers between devices with their start and end apart: 1, of which 1 were waited for; matrix products, arithmetic and copies ran while one was open for 0% of the time, Pallas kernels for 0%

profile of v1, /device:TPU:1, one launch (start us, length us, event | category | flops | bytes accessed | tf_op | source)
XLA Modules:
  0.0 99.8 jit_solution(15762279604424538356)
XLA Ops:
  0.0 0.8 copy.16.trans
  0.8 0.0 copy-start
  0.8 1.6 %copy-done = bf16[8,256,512]{2,1,0:T(8,128)(2,1)S(1)} copy-done((bf16[8,256,512]{2,1,0:T(8,128)(2,1)S(1)}, bf16[8,256,512]{2,1,0:T(8,128)(2,1)}, u32[]{:S(2)}) %copy-start) | copy-done | bytes 2097176
  2.3 0.0 copy-start.1
  2.3 1.1 %copy-done.1 = bf16[6,256,256]{2,1,0:T(8,128)(2,1)S(1)} copy-done((bf16[6,256,256]{2,1,0:T(8,128)(2,1)S(1)}, bf16[6,256,256]{2,1,0:T(8,128)(2,1)}, u32[]{:S(2)}) %copy-start.1) | copy-done | bytes 786456
  3.5 0.0 copy-start.2
  3.5 1.0 %copy-done.2 = bf16[512,512]{1,0:T(8,128)(2,1)S(1)} copy-done((bf16[512,512]{1,0:T(8,128)(2,1)S(1)}, bf16[512,512]{1,0:T(8,128)(2,1)}, u32[]{:S(2)}) %copy-start.2) | copy-done | bytes 524312
  4.5 0.0 copy-start.3
  4.5 1.0 %copy-done.3 = bf16[512,512]{1,0:T(8,128)(2,1)S(1)} copy-done((bf16[512,512]{1,0:T(8,128)(2,1)S(1)}, bf16[512,512]{1,0:T(8,128)(2,1)}, u32[]{:S(2)}) %copy-start.3) | copy-done | bytes 524312
  5.6 0.0 copy-start.8
  5.6 0.7 copy-done.8
  6.2 0.0 copy-start.9
  6.2 0.7 copy-done.9
  6.9 0.7 copy-done.10
  7.5 0.7 copy-done.11
  8.2 5.4 %front.1 = (bf16[8,384,128]{2,1,0:T(8,128)(2,1)S(1)}, bf16[8,384,128]{2,1,0:T(8,128)(2,1)S(1)}) custom-call(s32[8]{0:T(128)S(1)} %copy-done.8, s32[8]{0:T(128)S(1)} %copy-done.9, s32[8]{0:T(128)S(1)} %copy-done.10, f32[16,2]{1,0:T(8,128)S(1)} %copy.16.trans, f32[8]{0:T(128)S(1)} %copy-done.11, s32[1]{0:T(128)} %bitcast.core, ...), custom_call_target="tpu_custom_call" | custom-call | tf_op jit(solution)/shard_map/front/pallas_call | solution.py:180
  13.6 3.3 %collective-permute-start = (bf16[8,384,128]{2,1,0:T(8,128)(2,1)S(1)}, bf16[8,384,128]{2,1,0:T(8,128)(2,1)S(1)}, u32[]{:S(2)}, u32[]{:S(2)}) collective-permute-start(bf16[8,384,128]{2,1,0:T(8,128)(2,1)S(1)} %get-tuple-element.8), channel_id=1, source_target_pairs={{0,1},{1,0},{2,3},{3,2},{4,5},{5,4},{6,7},{7,6},{8,9},{9,8},{10,11... | collective-permute-start | bytes 2359304 | tf_op jit(solution)/shard_map/ppermute | solution.py:192
  16.9 1.9 %collective-permute-done = bf16[8,384,128]{2,1,0:T(8,128)(2,1)S(1)} collective-permute-done((bf16[8,384,128]{2,1,0:T(8,128)(2,1)S(1)}, bf16[8,384,128]{2,1,0:T(8,128)(2,1)S(1)}, u32[]{:S(2)}, u32[]{:S(2)}) %collective-permute-start) | collective-permute-done | bytes 786464 | tf_op jit(solution)/shard_map/ppermute | solution.py:192
  18.8 0.2 add_convert_fusion
  19.0 0.0 copy-start.4
  19.0 0.0 copy-start.5
  19.1 17.7 %all_to_all.20 = bf16[8,384,128]{2,1,0:T(8,128)(2,1)S(1)} all-to-all(bf16[8,384,128]{2,1,0:T(8,128)(2,1)S(1)} %add_convert_fusion), channel_id=1, replica_groups=mesh['xh'=2,'yy'=4,'zz'=8,'xl'=2,'co'=2] {'xh','yy'}, dimensions={0} | all-to-all | bytes 1572864 | tf_op jit(solution)/shard_map/all_to_all | solution.py:194
  36.7 0.1 reduce_sum.24
  36.8 16.4 %all_to_all.21 = bf16[16,24,128]{2,1,0:T(8,128)(2,1)S(1)} all-to-all(bf16[16,24,128]{2,1,0:T(8,128)(2,1)S(1)} %bitcast.6), channel_id=1, replica_groups=mesh['xh'=2,'yy'=4,'zz'=8,'xl'=2,'co'=2] {'zz','xl'}, dimensions={0} | all-to-all | bytes 196608 | tf_op jit(solution)/shard_map/all_to_all | solution.py:196
  53.3 16.8 %all_to_all.22.gathered = bf16[32,24,128]{2,1,0:T(8,128)(2,1)S(1)} all-to-all(bf16[32,24,128]{2,1,0:T(8,128)(2,1)S(1)} %broadcast_in_dim.2), channel_id=1, replica_groups=mesh['xh'=2,'yy'=4,'zz'=8,'xl'=2,'co'=2] {'zz','xl','co'}, dimensions={0} | all-to-all | bytes 393216 | tf_op jit(solution)/shard_map/all_to_all | solution.py:200
  70.1 0.0 copy-done.4
  70.1 0.0 copy-done.5
  70.1 7.2 %insert.1 = bf16[8,128,128]{2,1,0:T(8,128)(2,1)S(1)} custom-call(bf16[32,24,128]{2,1,0:T(8,128)(2,1)S(1)} %all_to_all.22.gathered, bf16[6,8,256,256]{3,2,1,0:T(8,128)(2,1)} %slab_rows.1, bf16[512,512]{1,0:T(8,128)(2,1)S(1)} %copy-done.5, bf16[512,512]{1,0:T(8,128)(2,1)S(1)} %copy-done.4), custom_call_target="tpu_custom_call" | custom-call | tf_op jit(solution)/shard_map/insert/pallas_call | solution.py:205
  77.3 21.4 %all_to_all.23 = bf16[256,4,128]{2,1,0:T(4,128)(2,1)S(1)} all-to-all(bf16[256,4,128]{2,1,0:T(4,128)(2,1)S(1)} %bitcast.5), channel_id=1, replica_groups=mesh['xh'=2,'yy'=4,'zz'=8,'xl'=2,'co'=2] {'xh','yy','zz','xl','co'}, dimensions={0} | all-to-all | bytes 524288 | tf_op jit(solution)/shard_map/all_to_all | solution.py:220
  98.7 0.0 copy-done.6
  98.7 0.0 copy-done.7
  98.7 1.1 %last.1 = f32[8,32,256]{2,1,0:T(8,128)} custom-call(bf16[8,128,128]{2,1,0:T(8,128)(2,1)S(1)} %bitcast.4, bf16[512,256]{1,0:T(8,128)(2,1)S(1)} %copy-done.7, bf16[512,256]{1,0:T(8,128)(2,1)S(1)} %copy-done.6), custom_call_target="tpu_custom_call" | custom-call | tf_op jit(solution)/shard_map/last/pallas_call | solution.py:224
  (6 shorter events, 0.1 us)
Async XLA Ops:
  0.8 1.6 %copy-start = (bf16[8,256,512]{2,1,0:T(8,128)(2,1)S(1)}, bf16[8,256,512]{2,1,0:T(8,128)(2,1)}, u32[]{:S(2)}) copy-start(bf16[8,256,512]{2,1,0:T(8,128)(2,1)} %images.1) | copy-start | bytes 6291460
  2.3 1.1 %copy-start.1 = (bf16[6,256,256]{2,1,0:T(8,128)(2,1)S(1)}, bf16[6,256,256]{2,1,0:T(8,128)(2,1)}, u32[]{:S(2)}) copy-start(bf16[6,256,256]{2,1,0:T(8,128)(2,1)} %in_plane.1) | copy-start | bytes 2359300
  3.5 1.0 %copy-start.2 = (bf16[512,512]{1,0:T(8,128)(2,1)S(1)}, bf16[512,512]{1,0:T(8,128)(2,1)}, u32[]{:S(2)}) copy-start(bf16[512,512]{1,0:T(8,128)(2,1)} %constant.21.clone.x_low) | copy-start | bytes 1572868
  4.5 1.0 %copy-start.3 = (bf16[512,512]{1,0:T(8,128)(2,1)S(1)}, bf16[512,512]{1,0:T(8,128)(2,1)}, u32[]{:S(2)}) copy-start(bf16[512,512]{1,0:T(8,128)(2,1)} %constant.20.clone.x_high) | copy-start | bytes 1572868
  5.6 0.7 copy-start.8
  6.2 0.7 copy-start.9
  6.9 0.7 copy-start.10
  7.5 0.7 copy-start.11
  13.6 5.2 %collective-permute-start = (bf16[8,384,128]{2,1,0:T(8,128)(2,1)S(1)}, bf16[8,384,128]{2,1,0:T(8,128)(2,1)S(1)}, u32[]{:S(2)}, u32[]{:S(2)}) collective-permute-start(bf16[8,384,128]{2,1,0:T(8,128)(2,1)S(1)} %get-tuple-element.8), channel_id=1, source_target_pairs={{0,1},{1,0},{2,3},{3,2},{4,5},{5,4},{6,7},{7,6},{8,9},{9,8},{10,11... | collective-permute-start | bytes 2359304 | tf_op jit(solution)/shard_map/ppermute | solution.py:192
  19.0 51.1 %copy-start.4 = (bf16[512,512]{1,0:T(8,128)(2,1)S(1)}, bf16[512,512]{1,0:T(8,128)(2,1)}, u32[]{:S(2)}) copy-start(bf16[512,512]{1,0:T(8,128)(2,1)} %constant.23.clone.y_low) | copy-start | bytes 1572868
  19.0 51.1 %copy-start.5 = (bf16[512,512]{1,0:T(8,128)(2,1)S(1)}, bf16[512,512]{1,0:T(8,128)(2,1)}, u32[]{:S(2)}) copy-start(bf16[512,512]{1,0:T(8,128)(2,1)} %constant.22.clone.y_high) | copy-start | bytes 1572868
  70.1 28.6 %copy-start.6 = (bf16[512,256]{1,0:T(8,128)(2,1)S(1)}, bf16[512,256]{1,0:T(8,128)(2,1)}, u32[]{:S(2)}) copy-start(bf16[512,256]{1,0:T(8,128)(2,1)} %constant.25.clone.z_low) | copy-start | bytes 786436
  70.1 28.6 %copy-start.7 = (bf16[512,256]{1,0:T(8,128)(2,1)S(1)}, bf16[512,256]{1,0:T(8,128)(2,1)}, u32[]{:S(2)}) copy-start(bf16[512,256]{1,0:T(8,128)(2,1)} %constant.24.clone.z_high) | copy-start | bytes 786436

commit v2 on v1

v2 whole, which is shorter than its diff:
```python
import math

import jax
import jax.numpy as jnp
import numpy as np
from jax import lax
from jax.experimental import pallas as pl
from jax.experimental.pallas import tpu as pltpu
from jax.sharding import Mesh
from jax.sharding import PartitionSpec as P

N = 256
ORIENT = 6
IMG = 8
BF16 = jnp.bfloat16
F32 = jnp.float32

DOM = ("xh", "yy")
SLAB = ("zz", "xl", "co")
ALL = DOM + SLAB


def split_table(table):
    high = table.astype(jnp.bfloat16)
    low = (table - high.astype(np.float64)).astype(jnp.bfloat16)
    return high, low


def phases(left, right):
    angles = (np.outer(left, right) % N) * (2.0 * math.pi / N)
    return np.cos(angles), np.sin(angles)


def x_table():
    x_of = (8 * np.arange(32)[None, :] + np.arange(8)[:, None]).reshape(-1)
    cosine, sine = (t.reshape(8, 32, N) for t in phases(x_of, np.arange(N)))
    real_rows = np.concatenate([cosine, -sine], axis=2)
    imag_rows = np.concatenate([sine, cosine], axis=2)
    return split_table(np.stack([real_rows, imag_rows], axis=1).reshape(512, 512))


def y_table():
    cosine, sine = (t.reshape(N, 8, 32) for t in phases(np.arange(N), np.arange(N)))
    from_real = np.stack([cosine, sine], axis=2).reshape(N, 512)
    from_imag = np.stack([-sine, cosine], axis=2).reshape(N, 512)
    return split_table(np.concatenate([from_real, from_imag], axis=0))


def z_table():
    half, slab, part = np.meshgrid(np.arange(2), np.arange(32), np.arange(4), indexing="ij")
    kz_of = (8 * slab + 4 * half + part).reshape(-1)
    cosine, sine = (t.reshape(2, 128, N) for t in phases(kz_of, np.arange(N)))
    return split_table(np.stack([cosine, -sine], axis=1).reshape(512, N))


def rows_dot(left, right):
    return lax.dot_general(left, right, (((1,), (1,)), ((), ())), preferred_element_type=F32)


def plain_dot(left, right):
    return jnp.dot(left, right, preferred_element_type=F32)


def front_kernel(
    scalars, images_hbm, in_plane_hbm, x_hbm,
    keep, send,
    total, images, in_plane, x_both, big_sems, image_sems,
):
    image_copies = [
        pltpu.make_async_copy(images_hbm.at[p], images.at[p], image_sems.at[p]) for p in range(IMG)
    ]
    for copy in image_copies:
        copy.start()
    plane_copy = pltpu.make_async_copy(in_plane_hbm, in_plane, big_sems.at[0])
    table_copy = pltpu.make_async_copy(x_hbm, x_both, big_sems.at[1])
    plane_copy.start()
    table_copy.start()
    total[...] = jnp.zeros_like(total)
    position = lax.broadcasted_iota(jnp.int32, (IMG, N), 1)
    freq = jnp.where(position < N // 2, position, position - N).astype(F32)
    row = lax.broadcasted_iota(jnp.int32, (IMG, N), 0)
    shift_y = jnp.zeros((IMG, N), F32)
    shift_x = jnp.zeros((IMG, N), F32)
    focus = jnp.zeros((IMG, N), F32)
    classes = []
    for p in range(IMG):
        code = scalars[p].astype(jnp.int32)
        shift, group = (code // 8) % 16, code // 128
        classes.append(code % 8)
        shift_y = jnp.where(row == p, scalars[8 + shift], shift_y)
        shift_x = jnp.where(row == p, scalars[24 + shift], shift_x)
        focus = jnp.where(row == p, scalars[40 + group], focus)
    squares = freq * freq * (1.0 / (N // 2) ** 2)
    step = 2.0 * math.pi / N
    angles = jnp.concatenate(
        [
            step * shift_y * freq,
            focus * squares + 0.1,
            step * shift_x * freq,
            focus * squares,
        ],
        axis=0,
    )
    sines = jnp.sin(angles)
    cosines = jnp.cos(angles)
    columns = jnp.concatenate([sines, cosines, jnp.zeros((64, N), F32)], axis=0).T
    chunk = 32
    for p in range(IMG):
        sin_tx, sin_fx = sines[16 + p : 17 + p], sines[24 + p : 25 + p]
        cos_tx, cos_fx = cosines[16 + p : 17 + p], cosines[24 + p : 25 + p]
        which = classes[p]
        image_copies[p].wait()
        for r in range(0, N, chunk):
            rows = slice(r, r + chunk)
            sin_ty = columns[rows, p : p + 1]
            sin_fy = columns[rows, 8 + p : 9 + p]
            cos_ty = columns[rows, 32 + p : 33 + p]
            cos_fy = columns[rows, 40 + p : 41 + p]
            contrast = -(sin_fy * cos_fx + cos_fy * sin_fx)
            turn_re = contrast * (cos_ty * cos_tx - sin_ty * sin_tx)
            turn_im = contrast * (sin_ty * cos_tx + cos_ty * sin_tx)
            real_part = images[p, rows, :N].astype(F32)
            imag_part = images[p, rows, N:].astype(F32)
            total[which, rows, :N] += real_part * turn_re + imag_part * turn_im
            total[which, rows, N:] += imag_part * turn_re - real_part * turn_im
    first = lax.axis_index("co") == 0
    plane_copy.wait()
    table_copy.wait()
    for o in range(ORIENT):
        sums = total[o].astype(BF16)
        matrix = in_plane[o]
        mixed = jnp.concatenate(
            [plain_dot(sums[:, :N], matrix), plain_dot(sums[:, N:], matrix)], axis=1
        ).astype(BF16)
        along = (rows_dot(x_both[0], mixed) + rows_dot(x_both[1], mixed)).astype(BF16)
        low_half, high_half = along[:, :128], along[:, 128:]
        own = jnp.where(first, low_half, high_half)
        other = jnp.where(first, high_half, low_half)
        for d in range(8):
            keep[d, 64 * o : 64 * o + 64, :] = own[64 * d : 64 * d + 64]
            send[d, 64 * o : 64 * o + 64, :] = other[64 * d : 64 * d + 64]


def insert_kernel(own, across, beside, corner, slab_hbm, y_both, out, rows_all, spectrum, slab_rows, sems):
    copies = [
        pltpu.make_async_copy(slab_hbm.at[:, plane], slab_rows.at[:, plane], sems.at[plane])
        for plane in range(8)
    ]
    for copy in copies:
        copy.start()
    side, core = lax.axis_index("xl"), lax.axis_index("co")
    rows_all[side, core] = own[...]
    rows_all[side, 1 - core] = across[...]
    rows_all[1 - side, core] = beside[...]
    rows_all[1 - side, 1 - core] = corner[...]
    for plane in range(8):
        copies[plane].wait()
        found = jnp.zeros((64, N), F32)
        for o in range(ORIENT):
            rows = slice(64 * (o % 3), 64 * (o % 3) + 64)
            factor = jnp.concatenate([rows_all[o // 3, c, rows, :] for c in range(2)], axis=1)
            found += rows_dot(factor, slab_rows[o, plane])
        start = (plane // 4) * 128 + plane % 4
        for part in range(4):
            rows, lanes = 32 * (part // 2), 128 * (part % 2)
            spectrum[part, pl.ds(start, 32, stride=4), :] = found[
                rows : rows + 32, lanes : lanes + 128
            ]
    lane = lax.broadcasted_iota(jnp.int32, (128, 128), 1)
    both = jnp.concatenate([spectrum[part] for part in range(4)], axis=1).astype(BF16)
    result = plain_dot(both, y_both[0]) + plain_dot(both, y_both[1])
    for e in range(4):
        early = result[:128, 128 * e : 128 * e + 128]
        late = result[128:, 128 * e : 128 * e + 128]
        even = jnp.where(lane < 64, early, pltpu.roll(late, 64, 1))
        odd = jnp.where(lane < 64, pltpu.roll(early, 64, 1), late)
        out[2 * e] = even.astype(BF16)
        out[2 * e + 1] = odd.astype(BF16)


def last_kernel(pencils, z_high, z_low, out):
    scaling = 1.0 / (N**1.5 * math.sqrt(2048))
    rows = []
    for d in range(8):
        turned = pencils[d].astype(F32).T.astype(BF16)
        rows.append(jnp.concatenate([turned[32 * q : 32 * q + 32] for q in range(4)], axis=1))
    stacked = jnp.concatenate(rows, axis=0)
    result = plain_dot(stacked, z_high[...]) + plain_dot(stacked, z_low[...])
    for d in range(8):
        out[d] = result[32 * d : 32 * d + 32] * scaling


VMEM_SPEC = pl.BlockSpec(memory_space=pltpu.VMEM)
SMEM_SPEC = pl.BlockSpec(memory_space=pltpu.SMEM)
HBM_SPEC = pl.BlockSpec(memory_space=pltpu.HBM)
FRONT_LIMIT = 53500 * 1024
INSERT_LIMIT = 53000 * 1024
LAST_LIMIT = 32768 * 1024


def swap(array, bits):
    return lax.ppermute(array, ("xl", "co"), [(i, i ^ bits) for i in range(4)])


def total_of(pieces):
    return jnp.sum(pieces.astype(F32), axis=0).astype(BF16)


def on_device(images, orient_ids, shift_ids, group_ids, translations, defocus, in_plane, slab_rows):
    codes = orient_ids + 8 * shift_ids + 128 * group_ids
    scalars = jnp.concatenate([codes.astype(F32), translations[:, 0], translations[:, 1], defocus])
    keep, send = pl.pallas_call(
        front_kernel,
        out_shape=[
            jax.ShapeDtypeStruct((8, 384, 128), BF16),
            jax.ShapeDtypeStruct((8, 384, 128), BF16),
        ],
        in_specs=[SMEM_SPEC] + [HBM_SPEC] * 3,
        out_specs=[VMEM_SPEC] * 2,
        scratch_shapes=[
            pltpu.VMEM((ORIENT, N, 2 * N), F32),
            pltpu.VMEM((IMG, N, 2 * N), BF16),
            pltpu.VMEM((ORIENT, N, N), BF16),
            pltpu.VMEM((2, 512, 512), BF16),
            pltpu.SemaphoreType.DMA((2,)),
            pltpu.SemaphoreType.DMA((IMG,)),
        ],
        compiler_params=pltpu.CompilerParams(vmem_limit_bytes=FRONT_LIMIT),
        name="front",
    )(
        scalars, images, in_plane, jnp.asarray(np.stack(x_table())),
    )
    other = lax.ppermute(send, "co", [(0, 1), (1, 0)])
    pair = (keep.astype(F32) + other.astype(F32)).astype(BF16)
    pieces = lax.all_to_all(
        pair.reshape(16, 192, 128), DOM + ("xl",), split_axis=0, concat_axis=0, tiled=True
    )
    part = total_of(pieces)
    pieces = lax.all_to_all(
        jnp.broadcast_to(part[None], (8, 192, 128)), "zz", split_axis=0, concat_axis=0, tiled=True
    )
    own = total_of(pieces)
    sent = pl.pallas_call(
        insert_kernel,
        out_shape=jax.ShapeDtypeStruct((8, 128, 128), BF16),
        in_specs=[VMEM_SPEC] * 4 + [HBM_SPEC, VMEM_SPEC],
        out_specs=VMEM_SPEC,
        scratch_shapes=[
            pltpu.VMEM((2, 2, 192, 128), BF16),
            pltpu.VMEM((4, N, 128), F32),
            pltpu.VMEM((ORIENT, 8, N, N), BF16),
            pltpu.SemaphoreType.DMA((8,)),
        ],
        compiler_params=pltpu.CompilerParams(vmem_limit_bytes=INSERT_LIMIT),
        name="insert",
    )(own, swap(own, 1), swap(own, 2), swap(own, 3), slab_rows, jnp.asarray(np.stack(y_table())))
    pencils = lax.all_to_all(
        sent.reshape(256, 4, 128), ALL, split_axis=0, concat_axis=0, tiled=True
    )
    z_high, z_low = z_table()
    return pl.pallas_call(
        last_kernel,
        out_shape=jax.ShapeDtypeStruct((8, 32, N), F32),
        in_specs=[VMEM_SPEC] * 3,
        out_specs=VMEM_SPEC,
        compiler_params=pltpu.CompilerParams(vmem_limit_bytes=LAST_LIMIT),
        name="last",
    )(pencils.reshape(8, 128, 128), jnp.asarray(z_high), jnp.asarray(z_low))


def solution(mesh):
    fine = Mesh(mesh.devices.reshape(2, 4, 8, 2, 2), ALL)
    return jax.shard_map(
        on_device,
        mesh=fine,
        in_specs=(
            P(ALL, None, None),
            P(ALL),
            P(ALL),
            P(ALL),
            P(),
            P(),
            P(),
            P(None, SLAB, None, None),
        ),
        out_specs=P(SLAB, DOM, None),
        check_vma=False,
    )
```

time: 100 us -> 89.1 us (0.89)
  blocking collectives: 72.3 us -> 60.2 us
  local copies, waits for them, and re-layouts: 8.23 us -> 0.83 us
  starting transfers between devices: 3.33 us -> 7.94 us
  waiting for transfers between devices: 1.91 us -> 4.63 us
  other arithmetic: 0.34 us -> 1.8 us
    all_to_all x3 -> x2, blocking collectives: 50.9 us -> 39.2 us  [the longest x1 20.6 us: on_device(): lax.all_to_all(jnp.broadcast_to(part[None], (8, 192, 128)), 'zz', split_a...]
    unnamed x25 -> x6, local copies, waits for them, and re-layouts: 8.2 us -> 0.02 us
    ppermute x0 -> x3, starting transfers between devices: none -> 4.62 us  [swap(): return lax.ppermute(array, ('xl', 'co'), [(i, i ^ bits) for i in range(4)])]
    ppermute x0 -> x3, waiting for transfers between devices: none -> 2.72 us  [swap(): return lax.ppermute(array, ('xl', 'co'), [(i, i ^ bits) for i in range(4)])]
    pallas_call x1, Pallas kernels: 7.18 us -> 5.96 us  [on_device(): pl.pallas_call(insert_kernel, out_shape=jax.ShapeDtypeStruct((8, 128, 128...]
    pallas_call x1, Pallas kernels: 5.38 us -> 6.44 us  [on_device(): pl.pallas_call(front_kernel, out_shape=[jax.ShapeDtypeStruct((8, 384, 128...]
  transfers between devices with their start and end apart: 1 -> 4, of which waited for: 1 -> 3; matrix products, arithmetic and copies ran while one was open for 0% -> 0% of each run, Pallas kernels for 0% -> 0%
where the time goes in v2:
time: 89.1 us; the launch traced here: 88.9 us
  blocking collectives  60.2 us (68%)
  Pallas kernels  13.5 us (15%)
  starting transfers between devices  7.94 us (9%)
  waiting for transfers between devices  4.63 us (5%)
  other arithmetic  1.8 us (2%)
    all_to_all x1, blocking collectives, on_device(): lax.all_to_all(sent.reshape(256, 4, 128), ALL, split_axis=0, concat_axis=...  21 us
    all_to_all x1, blocking collectives, on_device(): lax.all_to_all(jnp.broadcast_to(part[None], (8, 192, 128)), 'zz', split_a...  20.6 us
    all_to_all x1, blocking collectives, on_device(): lax.all_to_all(pair.reshape(16, 192, 128), DOM + ('xl',), split_axis=0, c...  18.6 us
    pallas_call x1, Pallas kernels, on_device(): pl.pallas_call(front_kernel, out_shape=[jax.ShapeDtypeStruct((8, 384, 128...  6.44 us
    pallas_call x1, Pallas kernels, on_device(): pl.pallas_call(insert_kernel, out_shape=jax.ShapeDtypeStruct((8, 128, 128...  5.96 us
    ppermute x3, starting transfers between devices, swap(): return lax.ppermute(array, ('xl', 'co'), [(i, i ^ bits) for i in range(4)])  4.62 us
    ppermute x1, starting transfers between devices, on_device(): other = lax.ppermute(send, 'co', [(0, 1), (1, 0)])  3.33 us
    ppermute x3, waiting for transfers between devices, swap(): return lax.ppermute(array, ('xl', 'co'), [(i, i ^ bits) for i in range(4)])  2.72 us
  transfers between devices with their start and end apart: 4, of which 3 were waited for; matrix products, arithmetic and copies ran while one was open for 0% of the time, Pallas kernels for 0%

profile of v2, /device:TPU:1, one launch (start us, length us, event | category | flops | bytes accessed | tf_op | source)
XLA Modules:
  0.0 88.9 jit_solution(7873771617432693672)
XLA Ops:
  0.0 0.8 slice_bitcast_fusion.1
  0.8 0.7 add_convert_fusion.1
  1.5 0.7 pad_maximum_fusion.scalars
  2.2 6.4 %front.1 = (bf16[8,384,128]{2,1,0:T(8,128)(2,1)S(1)}, bf16[8,384,128]{2,1,0:T(8,128)(2,1)S(1)}) custom-call(f32[48]{0:T(128)S(1)} %pad_maximum_fusion.scalars, bf16[8,256,512]{2,1,0:T(8,128)(2,1)} %images_hbm.1, bf16[6,256,256]{2,1,0:T(8,128)(2,1)} %in_plane_hbm.1, bf16[2,512,512]{2,1,0:T(8,128)(2,1)} %constant.16.clone.x_hbm), custom_call_target="tpu_custom_call" | custom-call | tf_op jit(solution)/shard_map/front/pallas_call | solution.py:212
  8.6 3.3 %collective-permute-start = (bf16[8,384,128]{2,1,0:T(8,128)(2,1)S(1)}, bf16[8,384,128]{2,1,0:T(8,128)(2,1)S(1)}, u32[]{:S(2)}, u32[]{:S(2)}) collective-permute-start(bf16[8,384,128]{2,1,0:T(8,128)(2,1)S(1)} %get-tuple-element.8), channel_id=1, source_target_pairs={{0,1},{1,0},{2,3},{3,2},{4,5},{5,4},{6,7},{7,6},{8,9},{9,8},{10,11... | collective-permute-start | bytes 2359304 | tf_op jit(solution)/shard_map/ppermute | solution.py:233
  12.0 1.9 %collective-permute-done = bf16[8,384,128]{2,1,0:T(8,128)(2,1)S(1)} collective-permute-done((bf16[8,384,128]{2,1,0:T(8,128)(2,1)S(1)}, bf16[8,384,128]{2,1,0:T(8,128)(2,1)S(1)}, u32[]{:S(2)}, u32[]{:S(2)}) %collective-permute-start) | collective-permute-done | bytes 786464 | tf_op jit(solution)/shard_map/ppermute | solution.py:233
  13.9 0.2 add_convert_fusion
  14.1 18.6 %all_to_all.15 = bf16[16,192,128]{2,1,0:T(8,128)(2,1)S(1)} all-to-all(bf16[16,192,128]{2,1,0:T(8,128)(2,1)S(1)} %bitcast.9), channel_id=1, replica_groups=mesh['xh'=2,'yy'=4,'zz'=8,'xl'=2,'co'=2] {'xh','yy','xl'}, dimensions={0} | all-to-all | bytes 1572864 | tf_op jit(solution)/shard_map/all_to_all | solution.py:235
  32.7 0.0 copy-start
  32.7 0.1 reduce_sum.24
  32.8 0.1 broadcast_in_dim.2
  32.9 20.6 %all_to_all.16 = bf16[8,192,128]{2,1,0:T(8,128)(2,1)S(1)} all-to-all(bf16[8,192,128]{2,1,0:T(8,128)(2,1)S(1)} %broadcast_in_dim.2), channel_id=1, replica_groups=mesh['xh'=2,'yy'=4,'zz'=8,'xl'=2,'co'=2] {'zz'}, dimensions={0} | all-to-all | bytes 786432 | tf_op jit(solution)/shard_map/all_to_all | solution.py:239
  53.5 0.1 reduce_sum.25.own
  53.5 0.0 copy-start.1
  53.5 0.0 copy-start.2
  53.6 3.4 %collective-permute-start.3 = (bf16[192,128]{1,0:T(8,128)(2,1)S(1)}, bf16[192,128]{1,0:T(8,128)(2,1)S(1)}, u32[]{:S(2)}, u32[]{:S(2)}) collective-permute-start(bf16[192,128]{1,0:T(8,128)(2,1)S(1)} %reduce_sum.25.own), channel_id=1, source_target_pairs={{0,3},{1,2},{2,1},{3,0},{4,7},{5,6},{6,5},{7,4},{8,11},{9,10},{10,... | collective-permute-start | bytes 147464 | tf_op jit(solution)/shard_map/ppermute | solution.py:202
  57.0 1.2 %collective-permute-start.2 = (bf16[192,128]{1,0:T(8,128)(2,1)S(1)}, bf16[192,128]{1,0:T(8,128)(2,1)S(1)}, u32[]{:S(2)}, u32[]{:S(2)}) collective-permute-start(bf16[192,128]{1,0:T(8,128)(2,1)S(1)} %reduce_sum.25.own), channel_id=1, source_target_pairs={{0,2},{1,3},{2,0},{3,1},{4,6},{5,7},{6,4},{7,5},{8,10},{9,11},{10,... | collective-permute-start | bytes 147464 | tf_op jit(solution)/shard_map/ppermute | solution.py:202
  58.2 0.0 collective-permute-start.1
  58.2 0.6 collective-permute-done.3.corner
  58.8 2.1 %collective-permute-done.2.beside = bf16[192,128]{1,0:T(8,128)(2,1)S(1)} collective-permute-done((bf16[192,128]{1,0:T(8,128)(2,1)S(1)}, bf16[192,128]{1,0:T(8,128)(2,1)S(1)}, u32[]{:S(2)}, u32[]{:S(2)}) %collective-permute-start.2) | collective-permute-done | bytes 49184 | tf_op jit(solution)/shard_map/ppermute | solution.py:202
  60.9 0.0 collective-permute-done.1.across
  60.9 0.0 copy-done
  60.9 6.0 %insert.1 = bf16[8,128,128]{2,1,0:T(8,128)(2,1)S(1)} custom-call(bf16[192,128]{1,0:T(8,128)(2,1)S(1)} %reduce_sum.25.own, bf16[192,128]{1,0:T(8,128)(2,1)S(1)} %collective-permute-done.1.across, bf16[192,128]{1,0:T(8,128)(2,1)S(1)} %collective-permute-done.2.beside, bf16[192,128]{1,0:T(8,128)(2,1)S(1)} %collective-permute-done.3.corner, ...), custom_call_target="tpu_custom_call" | custom-call | tf_op jit(solution)/shard_map/insert/pallas_call | solution.py:243
  66.9 21.0 %all_to_all.17 = bf16[256,4,128]{2,1,0:T(4,128)(2,1)S(1)} all-to-all(bf16[256,4,128]{2,1,0:T(4,128)(2,1)S(1)} %bitcast.8), channel_id=1, replica_groups=mesh['xh'=2,'yy'=4,'zz'=8,'xl'=2,'co'=2] {'xh','yy','zz','xl','co'}, dimensions={0} | all-to-all | bytes 524288 | tf_op jit(solution)/shard_map/all_to_all | solution.py:257
  87.8 0.0 copy-done.1
  87.9 0.0 copy-done.2
  87.9 1.1 %last.1 = f32[8,32,256]{2,1,0:T(8,128)} custom-call(bf16[8,128,128]{2,1,0:T(8,128)(2,1)S(1)} %bitcast.7, bf16[512,256]{1,0:T(8,128)(2,1)S(1)} %copy-done.2, bf16[512,256]{1,0:T(8,128)(2,1)S(1)} %copy-done.1), custom_call_target="tpu_custom_call" | custom-call | tf_op jit(solution)/shard_map/last/pallas_call | solution.py:261
Async XLA Ops:
  8.6 5.2 %collective-permute-start = (bf16[8,384,128]{2,1,0:T(8,128)(2,1)S(1)}, bf16[8,384,128]{2,1,0:T(8,128)(2,1)S(1)}, u32[]{:S(2)}, u32[]{:S(2)}) collective-permute-start(bf16[8,384,128]{2,1,0:T(8,128)(2,1)S(1)} %get-tuple-element.8), channel_id=1, source_target_pairs={{0,1},{1,0},{2,3},{3,2},{4,5},{5,4},{6,7},{7,6},{8,9},{9,8},{10,11... | collective-permute-start | bytes 2359304 | tf_op jit(solution)/shard_map/ppermute | solution.py:233
  32.7 28.2 %copy-start = (bf16[2,512,512]{2,1,0:T(8,128)(2,1)S(1)}, bf16[2,512,512]{2,1,0:T(8,128)(2,1)}, u32[]{:S(2)}) copy-start(bf16[2,512,512]{2,1,0:T(8,128)(2,1)} %constant.17.clone.y_both) | copy-start | bytes 3145732
  53.5 34.3 %copy-start.1 = (bf16[512,256]{1,0:T(8,128)(2,1)S(1)}, bf16[512,256]{1,0:T(8,128)(2,1)}, u32[]{:S(2)}) copy-start(bf16[512,256]{1,0:T(8,128)(2,1)} %constant.19.clone.z_low) | copy-start | bytes 786436
  53.5 34.3 %copy-start.2 = (bf16[512,256]{1,0:T(8,128)(2,1)S(1)}, bf16[512,256]{1,0:T(8,128)(2,1)}, u32[]{:S(2)}) copy-start(bf16[512,256]{1,0:T(8,128)(2,1)} %constant.18.clone.z_high) | copy-start | bytes 786436
  53.6 5.2 %collective-permute-start.3 = (bf16[192,128]{1,0:T(8,128)(2,1)S(1)}, bf16[192,128]{1,0:T(8,128)(2,1)S(1)}, u32[]{:S(2)}, u32[]{:S(2)}) collective-permute-start(bf16[192,128]{1,0:T(8,128)(2,1)S(1)} %reduce_sum.25.own), channel_id=1, source_target_pairs={{0,3},{1,2},{2,1},{3,0},{4,7},{5,6},{6,5},{7,4},{8,11},{9,10},{10,... | collective-permute-start | bytes 147464 | tf_op jit(solution)/shard_map/ppermute | solution.py:202
  57.0 3.9 %collective-permute-start.2 = (bf16[192,128]{1,0:T(8,128)(2,1)S(1)}, bf16[192,128]{1,0:T(8,128)(2,1)S(1)}, u32[]{:S(2)}, u32[]{:S(2)}) collective-permute-start(bf16[192,128]{1,0:T(8,128)(2,1)S(1)} %reduce_sum.25.own), channel_id=1, source_target_pairs={{0,2},{1,3},{2,0},{3,1},{4,6},{5,7},{6,4},{7,5},{8,10},{9,11},{10,... | collective-permute-start | bytes 147464 | tf_op jit(solution)/shard_map/ppermute | solution.py:202
  58.2 2.7 %collective-permute-start.1 = (bf16[192,128]{1,0:T(8,128)(2,1)S(1)}, bf16[192,128]{1,0:T(8,128)(2,1)S(1)}, u32[]{:S(2)}, u32[]{:S(2)}) collective-permute-start(bf16[192,128]{1,0:T(8,128)(2,1)S(1)} %reduce_sum.25.own), channel_id=1, source_target_pairs={{0,1},{1,0},{2,3},{3,2},{4,5},{5,4},{6,7},{7,6},{8,9},{9,8},{10,11... | collective-permute-start | bytes 147464 | tf_op jit(solution)/shard_map/ppermute | solution.py:202

commit v3 on v2

--- a/solution.py
+++ b/solution.py
@@ -62,9 +62,9 @@
 
 
 def front_kernel(
-    scalars, images_hbm, in_plane_hbm, x_hbm,
+    scalars, images_hbm, in_plane_hbm, tables,
     keep, send,
-    total, images, in_plane, x_both, big_sems, image_sems,
+    total, images, in_plane, x_rows, big_sems, image_sems,
 ):
     image_copies = [
         pltpu.make_async_copy(images_hbm.at[p], images.at[p], image_sems.at[p]) for p in range(IMG)
@@ -72,9 +72,7 @@
     for copy in image_copies:
         copy.start()
     plane_copy = pltpu.make_async_copy(in_plane_hbm, in_plane, big_sems.at[0])
-    table_copy = pltpu.make_async_copy(x_hbm, x_both, big_sems.at[1])
-    plane_copy.start()
-    table_copy.start()
+    table_copy = pltpu.make_async_copy(tables.at[0], x_rows, big_sems.at[1])
     total[...] = jnp.zeros_like(total)
     position = lax.broadcasted_iota(jnp.int32, (IMG, N), 1)
     freq = jnp.where(position < N // 2, position, position - N).astype(F32)
@@ -84,12 +82,12 @@
     focus = jnp.zeros((IMG, N), F32)
     classes = []
     for p in range(IMG):
-        code = scalars[p].astype(jnp.int32)
+        code = scalars[0, 16 + p].astype(jnp.int32)
         shift, group = (code // 8) % 16, code // 128
         classes.append(code % 8)
-        shift_y = jnp.where(row == p, scalars[8 + shift], shift_y)
-        shift_x = jnp.where(row == p, scalars[24 + shift], shift_x)
-        focus = jnp.where(row == p, scalars[40 + group], focus)
+        shift_y = jnp.where(row == p, scalars[0, shift], shift_y)
+        shift_x = jnp.where(row == p, scalars[1, shift], shift_x)
+        focus = jnp.where(row == p, scalars[0, 24 + group], focus)
     squares = freq * freq * (1.0 / (N // 2) ** 2)
     step = 2.0 * math.pi / N
     angles = jnp.concatenate(
@@ -104,12 +102,15 @@
     sines = jnp.sin(angles)
     cosines = jnp.cos(angles)
     columns = jnp.concatenate([sines, cosines, jnp.zeros((64, N), F32)], axis=0).T
+    for copy in image_copies:
+        copy.wait()
+    plane_copy.start()
+    table_copy.start()
     chunk = 32
     for p in range(IMG):
         sin_tx, sin_fx = sines[16 + p : 17 + p], sines[24 + p : 25 + p]
         cos_tx, cos_fx = cosines[16 + p : 17 + p], cosines[24 + p : 25 + p]
         which = classes[p]
-        image_copies[p].wait()
         for r in range(0, N, chunk):
             rows = slice(r, r + chunk)
             sin_ty = columns[rows, p : p + 1]
@@ -132,7 +133,7 @@
         mixed = jnp.concatenate(
             [plain_dot(sums[:, :N], matrix), plain_dot(sums[:, N:], matrix)], axis=1
         ).astype(BF16)
-        along = (rows_dot(x_both[0], mixed) + rows_dot(x_both[1], mixed)).astype(BF16)
+        along = rows_dot(x_rows[...], mixed).astype(BF16)
         low_half, high_half = along[:, :128], along[:, 128:]
         own = jnp.where(first, low_half, high_half)
         other = jnp.where(first, high_half, low_half)
@@ -141,20 +142,24 @@
             send[d, 64 * o : 64 * o + 64, :] = other[64 * d : 64 * d + 64]
 
 
-def insert_kernel(own, across, beside, corner, slab_hbm, y_both, out, rows_all, spectrum, slab_rows, sems):
+def fetch_kernel(after, slab_hbm, slab_rows, sems):
+    del after
     copies = [
-        pltpu.make_async_copy(slab_hbm.at[:, plane], slab_rows.at[:, plane], sems.at[plane])
-        for plane in range(8)
+        pltpu.make_async_copy(slab_hbm.at[o], slab_rows.at[o], sems.at[o]) for o in range(ORIENT)
     ]
     for copy in copies:
         copy.start()
+    for copy in copies:
+        copy.wait()
+
+
+def insert_kernel(own, across, beside, corner, slab_rows, tables, out, rows_all, spectrum):
     side, core = lax.axis_index("xl"), lax.axis_index("co")
     rows_all[side, core] = own[...]
     rows_all[side, 1 - core] = across[...]
     rows_all[1 - side, core] = beside[...]
     rows_all[1 - side, 1 - core] = corner[...]
     for plane in range(8):
-        copies[plane].wait()
         found = jnp.zeros((64, N), F32)
         for o in range(ORIENT):
             rows = slice(64 * (o % 3), 64 * (o % 3) + 64)
@@ -168,7 +173,7 @@
             ]
     lane = lax.broadcasted_iota(jnp.int32, (128, 128), 1)
     both = jnp.concatenate([spectrum[part] for part in range(4)], axis=1).astype(BF16)
-    result = plain_dot(both, y_both[0]) + plain_dot(both, y_both[1])
+    result = plain_dot(both, tables[1]) + plain_dot(both, tables[2])
     for e in range(4):
         early = result[:128, 128 * e : 128 * e + 128]
         late = result[128:, 128 * e : 128 * e + 128]
@@ -194,7 +199,8 @@
 SMEM_SPEC = pl.BlockSpec(memory_space=pltpu.SMEM)
 HBM_SPEC = pl.BlockSpec(memory_space=pltpu.HBM)
 FRONT_LIMIT = 53500 * 1024
-INSERT_LIMIT = 53000 * 1024
+FETCH_LIMIT = 44000 * 1024
+INSERT_LIMIT = 44000 * 1024
 LAST_LIMIT = 32768 * 1024
 
 
@@ -207,8 +213,13 @@
 
 
 def on_device(images, orient_ids, shift_ids, group_ids, translations, defocus, in_plane, slab_rows):
+    tables = jnp.asarray(np.stack([x_table()[0], *y_table()]))
     codes = orient_ids + 8 * shift_ids + 128 * group_ids
-    scalars = jnp.concatenate([codes.astype(F32), translations[:, 0], translations[:, 1], defocus])
+    scalars = (
+        jnp.pad(translations.T, ((0, 0), (0, 16)))
+        + jnp.pad(codes.astype(F32)[None], ((0, 1), (16, 8)))
+        + jnp.pad(defocus[None], ((0, 1), (24, 0)))
+    )
     keep, send = pl.pallas_call(
         front_kernel,
         out_shape=[
@@ -221,14 +232,14 @@
             pltpu.VMEM((ORIENT, N, 2 * N), F32),
             pltpu.VMEM((IMG, N, 2 * N), BF16),
             pltpu.VMEM((ORIENT, N, N), BF16),
-            pltpu.VMEM((2, 512, 512), BF16),
+            pltpu.VMEM((512, 512), BF16),
             pltpu.SemaphoreType.DMA((2,)),
             pltpu.SemaphoreType.DMA((IMG,)),
         ],
         compiler_params=pltpu.CompilerParams(vmem_limit_bytes=FRONT_LIMIT),
         name="front",
     )(
-        scalars, images, in_plane, jnp.asarray(np.stack(x_table())),
+        scalars, images, in_plane, tables,
     )
     other = lax.ppermute(send, "co", [(0, 1), (1, 0)])
     pair = (keep.astype(F32) + other.astype(F32)).astype(BF16)
@@ -240,20 +251,28 @@
         jnp.broadcast_to(part[None], (8, 192, 128)), "zz", split_axis=0, concat_axis=0, tiled=True
     )
     own = total_of(pieces)
+    fetched = pl.pallas_call(
+        fetch_kernel,
+        out_shape=jax.ShapeDtypeStruct(slab_rows.shape, BF16),
+        in_specs=[VMEM_SPEC, HBM_SPEC],
+        out_specs=VMEM_SPEC,
+        scratch_shapes=[pltpu.SemaphoreType.DMA((ORIENT,))],
+        compiler_params=pltpu.CompilerParams(vmem_limit_bytes=FETCH_LIMIT),
+        cost_estimate=pl.CostEstimate(flops=0, bytes_accessed=12_000_000, transcendentals=0),
+        name="fetch",
+    )(own, slab_rows)
     sent = pl.pallas_call(
         insert_kernel,
         out_shape=jax.ShapeDtypeStruct((8, 128, 128), BF16),
-        in_specs=[VMEM_SPEC] * 4 + [HBM_SPEC, VMEM_SPEC],
+        in_specs=[VMEM_SPEC] * 6,
         out_specs=VMEM_SPEC,
         scratch_shapes=[
             pltpu.VMEM((2, 2, 192, 128), BF16),
             pltpu.VMEM((4, N, 128), F32),
-            pltpu.VMEM((ORIENT, 8, N, N), BF16),
-            pltpu.SemaphoreType.DMA((8,)),
         ],
         compiler_params=pltpu.CompilerParams(vmem_limit_bytes=INSERT_LIMIT),
         name="insert",
-    )(own, swap(own, 1), swap(own, 2), swap(own, 3), slab_rows, jnp.asarray(np.stack(y_table())))
+    )(own, swap(own, 1), swap(own, 2), swap(own, 3), fetched, tables)
     pencils = lax.all_to_all(
         sent.reshape(256, 4, 128), ALL, split_axis=0, concat_axis=0, tiled=True
     )

time: 89.1 us -> 84.1 us (0.944)
  waiting for transfers between devices: 4.63 us -> 1.92 us
  Pallas kernels: 13.5 us -> 11.9 us
    pallas_call x1, Pallas kernels: 5.96 us -> 2.44 us  [on_device(): pl.pallas_call(insert_kernel, out_shape=jax.ShapeDtypeStruct((8, 128, 128...]
    pallas_call x0 -> x1, Pallas kernels: none -> 2.85 us  [on_device(): pl.pallas_call(fetch_kernel, out_shape=jax.ShapeDtypeStruct(slab_rows.sha...]
    ppermute x3, waiting for transfers between devices: 2.72 us -> 0.01 us  [swap(): return lax.ppermute(array, ('xl', 'co'), [(i, i ^ bits) for i in range(4)])]
  transfers between devices with their start and end apart: 4 -> 4, of which waited for: 3 -> 1; matrix products, arithmetic and copies ran while one was open for 0% -> 0% of each run, Pallas kernels for 0% -> 3%
where the time goes in v3:
time: 84.1 us; the launch traced here: 83.9 us
  blocking collectives  60.1 us (71%)
  Pallas kernels  11.9 us (14%)
  starting transfers between devices  7.94 us (9%)
  waiting for transfers between devices  1.92 us (2%)
  other arithmetic  1.84 us (2%)
    all_to_all x1, blocking collectives, on_device(): lax.all_to_all(sent.reshape(256, 4, 128), ALL, split_axis=0, concat_axis=...  21 us
    all_to_all x1, blocking collectives, on_device(): lax.all_to_all(jnp.broadcast_to(part[None], (8, 192, 128)), 'zz', split_a...  20.4 us
    all_to_all x1, blocking collectives, on_device(): lax.all_to_all(pair.reshape(16, 192, 128), DOM + ('xl',), split_axis=0, c...  18.6 us
    pallas_call x1, Pallas kernels, on_device(): pl.pallas_call(front_kernel, out_shape=[jax.ShapeDtypeStruct((8, 384, 128...  5.57 us
    ppermute x3, starting transfers between devices, swap(): return lax.ppermute(array, ('xl', 'co'), [(i, i ^ bits) for i in range(4)])  4.62 us
    ppermute x1, starting transfers between devices, on_device(): other = lax.ppermute(send, 'co', [(0, 1), (1, 0)])  3.32 us
    pallas_call x1, Pallas kernels, on_device(): pl.pallas_call(fetch_kernel, out_shape=jax.ShapeDtypeStruct(slab_rows.sha...  2.85 us
    pallas_call x1, Pallas kernels, on_device(): pl.pallas_call(insert_kernel, out_shape=jax.ShapeDtypeStruct((8, 128, 128...  2.44 us
  transfers between devices with their start and end apart: 4, of which 1 were waited for; matrix products, arithmetic and copies ran while one was open for 0% of the time, Pallas kernels for 3%

profile of v3, /device:TPU:1, one launch (start us, length us, event | category | flops | bytes accessed | tf_op | source)
XLA Modules:
  0.0 83.9 jit_solution(15210378195415897916)
XLA Ops:
  0.0 0.7 convert_bitcast_fusion
  0.7 0.8 pad_add_fusion.scalars
  1.5 5.6 %front.1 = (bf16[8,384,128]{2,1,0:T(8,128)(2,1)S(1)}, bf16[8,384,128]{2,1,0:T(8,128)(2,1)S(1)}) custom-call(f32[2,32]{1,0:T(2,128)S(1)} %pad_add_fusion.scalars, bf16[8,256,512]{2,1,0:T(8,128)(2,1)} %images_hbm.1, bf16[6,256,256]{2,1,0:T(8,128)(2,1)} %in_plane_hbm.1, bf16[3,512,512]{2,1,0:T(8,128)(2,1)} %constant.17.clone.tables), custom_call_target="tpu_custom_call" | custom-call | tf_op jit(solution)/shard_map/front/pallas_call | solution.py:223
  7.0 3.3 %collective-permute-start = (bf16[8,384,128]{2,1,0:T(8,128)(2,1)S(1)}, bf16[8,384,128]{2,1,0:T(8,128)(2,1)S(1)}, u32[]{:S(2)}, u32[]{:S(2)}) collective-permute-start(bf16[8,384,128]{2,1,0:T(8,128)(2,1)S(1)} %get-tuple-element.8), channel_id=1, source_target_pairs={{0,1},{1,0},{2,3},{3,2},{4,5},{5,4},{6,7},{7,6},{8,9},{9,8},{10,11... | collective-permute-start | bytes 2359304 | tf_op jit(solution)/shard_map/ppermute | solution.py:244
  10.4 1.9 %collective-permute-done = bf16[8,384,128]{2,1,0:T(8,128)(2,1)S(1)} collective-permute-done((bf16[8,384,128]{2,1,0:T(8,128)(2,1)S(1)}, bf16[8,384,128]{2,1,0:T(8,128)(2,1)S(1)}, u32[]{:S(2)}, u32[]{:S(2)}) %collective-permute-start) | collective-permute-done | bytes 786464 | tf_op jit(solution)/shard_map/ppermute | solution.py:244
  12.3 0.2 add_convert_fusion
  12.5 18.6 %all_to_all.15 = bf16[16,192,128]{2,1,0:T(8,128)(2,1)S(1)} all-to-all(bf16[16,192,128]{2,1,0:T(8,128)(2,1)S(1)} %bitcast.9), channel_id=1, replica_groups=mesh['xh'=2,'yy'=4,'zz'=8,'xl'=2,'co'=2] {'xh','yy','xl'}, dimensions={0} | all-to-all | bytes 1572864 | tf_op jit(solution)/shard_map/all_to_all | solution.py:246
  31.1 0.1 reduce_sum.24
  31.2 0.1 broadcast_in_dim.14
  31.3 20.4 %all_to_all.16 = bf16[8,192,128]{2,1,0:T(8,128)(2,1)S(1)} all-to-all(bf16[8,192,128]{2,1,0:T(8,128)(2,1)S(1)} %broadcast_in_dim.14), channel_id=1, replica_groups=mesh['xh'=2,'yy'=4,'zz'=8,'xl'=2,'co'=2] {'zz'}, dimensions={0} | all-to-all | bytes 786432 | tf_op jit(solution)/shard_map/all_to_all | solution.py:250
  51.7 0.1 reduce_sum.25.after.own
  51.8 0.0 copy-start
  51.8 3.4 %collective-permute-start.3 = (bf16[192,128]{1,0:T(8,128)(2,1)S(1)}, bf16[192,128]{1,0:T(8,128)(2,1)S(1)}, u32[]{:S(2)}, u32[]{:S(2)}) collective-permute-start(bf16[192,128]{1,0:T(8,128)(2,1)S(1)} %reduce_sum.25.after.own), channel_id=1, source_target_pairs={{0,3},{1,2},{2,1},{3,0},{4,7},{5,6},{6,5},{7,4},{8,11},{9,10},{10,... | collective-permute-start | bytes 147464 | tf_op jit(solution)/shard_map/ppermute | solution.py:208
  55.2 1.2 %collective-permute-start.2 = (bf16[192,128]{1,0:T(8,128)(2,1)S(1)}, bf16[192,128]{1,0:T(8,128)(2,1)S(1)}, u32[]{:S(2)}, u32[]{:S(2)}) collective-permute-start(bf16[192,128]{1,0:T(8,128)(2,1)S(1)} %reduce_sum.25.after.own), channel_id=1, source_target_pairs={{0,2},{1,3},{2,0},{3,1},{4,6},{5,7},{6,4},{7,5},{8,10},{9,11},{10,... | collective-permute-start | bytes 147464 | tf_op jit(solution)/shard_map/ppermute | solution.py:208
  56.4 0.0 collective-permute-start.1
  56.4 2.9 %fetch.1.slab_rows = bf16[6,8,256,256]{3,2,1,0:T(8,128)(2,1)S(1)} custom-call(bf16[192,128]{1,0:T(8,128)(2,1)S(1)} %reduce_sum.25.after.own, bf16[6,8,256,256]{3,2,1,0:T(8,128)(2,1)} %slab_hbm.1), custom_call_target="tpu_custom_call" | custom-call | bytes 12000000 | tf_op jit(solution)/shard_map/fetch/pallas_call | solution.py:254
  59.3 0.0 copy-start.1
  59.3 0.0 copy-start.2
  59.3 0.0 collective-permute-done.3.corner
  59.3 0.0 collective-permute-done.2.beside
  59.3 0.0 collective-permute-done.1.across
  59.3 0.0 copy-done
  59.4 2.4 %insert.1 = bf16[8,128,128]{2,1,0:T(8,128)(2,1)S(1)} custom-call(bf16[192,128]{1,0:T(8,128)(2,1)S(1)} %reduce_sum.25.after.own, bf16[192,128]{1,0:T(8,128)(2,1)S(1)} %collective-permute-done.1.across, bf16[192,128]{1,0:T(8,128)(2,1)S(1)} %collective-permute-done.2.beside, bf16[192,128]{1,0:T(8,128)(2,1)S(1)} %collective-permute-done.3.corner, ...), custom_call_target="tpu_custom_call" | custom-call | tf_op jit(solution)/shard_map/insert/pallas_call | solution.py:264
  61.8 21.0 %all_to_all.17 = bf16[256,4,128]{2,1,0:T(4,128)(2,1)S(1)} all-to-all(bf16[256,4,128]{2,1,0:T(4,128)(2,1)S(1)} %bitcast.7), channel_id=1, replica_groups=mesh['xh'=2,'yy'=4,'zz'=8,'xl'=2,'co'=2] {'xh','yy','zz','xl','co'}, dimensions={0} | all-to-all | bytes 524288 | tf_op jit(solution)/shard_map/all_to_all | solution.py:276
  82.8 0.0 copy-done.1
  82.8 0.0 copy-done.2
  82.8 1.1 %last.1 = f32[8,32,256]{2,1,0:T(8,128)} custom-call(bf16[8,128,128]{2,1,0:T(8,128)(2,1)S(1)} %bitcast.8, bf16[512,256]{1,0:T(8,128)(2,1)S(1)} %copy-done.2, bf16[512,256]{1,0:T(8,128)(2,1)S(1)} %copy-done.1), custom_call_target="tpu_custom_call" | custom-call | tf_op jit(solution)/shard_map/last/pallas_call | solution.py:280
Async XLA Ops:
  7.0 5.2 %collective-permute-start = (bf16[8,384,128]{2,1,0:T(8,128)(2,1)S(1)}, bf16[8,384,128]{2,1,0:T(8,128)(2,1)S(1)}, u32[]{:S(2)}, u32[]{:S(2)}) collective-permute-start(bf16[8,384,128]{2,1,0:T(8,128)(2,1)S(1)} %get-tuple-element.8), channel_id=1, source_target_pairs={{0,1},{1,0},{2,3},{3,2},{4,5},{5,4},{6,7},{7,6},{8,9},{9,8},{10,11... | collective-permute-start | bytes 2359304 | tf_op jit(solution)/shard_map/ppermute | solution.py:244
  51.8 7.5 %copy-start = (bf16[3,512,512]{2,1,0:T(8,128)(2,1)S(1)}, bf16[3,512,512]{2,1,0:T(8,128)(2,1)}, u32[]{:S(2)}) copy-start(bf16[3,512,512]{2,1,0:T(8,128)(2,1)} %constant.17.clone.tables) | copy-start | bytes 4718596
  51.8 7.5 %collective-permute-start.3 = (bf16[192,128]{1,0:T(8,128)(2,1)S(1)}, bf16[192,128]{1,0:T(8,128)(2,1)S(1)}, u32[]{:S(2)}, u32[]{:S(2)}) collective-permute-start(bf16[192,128]{1,0:T(8,128)(2,1)S(1)} %reduce_sum.25.after.own), channel_id=1, source_target_pairs={{0,3},{1,2},{2,1},{3,0},{4,7},{5,6},{6,5},{7,4},{8,11},{9,10},{10,... | collective-permute-start | bytes 147464 | tf_op jit(solution)/shard_map/ppermute | solution.py:208
  55.2 4.1 %collective-permute-start.2 = (bf16[192,128]{1,0:T(8,128)(2,1)S(1)}, bf16[192,128]{1,0:T(8,128)(2,1)S(1)}, u32[]{:S(2)}, u32[]{:S(2)}) collective-permute-start(bf16[192,128]{1,0:T(8,128)(2,1)S(1)} %reduce_sum.25.after.own), channel_id=1, source_target_pairs={{0,2},{1,3},{2,0},{3,1},{4,6},{5,7},{6,4},{7,5},{8,10},{9,11},{10,... | collective-permute-start | bytes 147464 | tf_op jit(solution)/shard_map/ppermute | solution.py:208
  56.4 2.9 %collective-permute-start.1 = (bf16[192,128]{1,0:T(8,128)(2,1)S(1)}, bf16[192,128]{1,0:T(8,128)(2,1)S(1)}, u32[]{:S(2)}, u32[]{:S(2)}) collective-permute-start(bf16[192,128]{1,0:T(8,128)(2,1)S(1)} %reduce_sum.25.after.own), channel_id=1, source_target_pairs={{0,1},{1,0},{2,3},{3,2},{4,5},{5,4},{6,7},{7,6},{8,9},{9,8},{10,11... | collective-permute-start | bytes 147464 | tf_op jit(solution)/shard_map/ppermute | solution.py:208
  59.3 23.5 %copy-start.1 = (bf16[512,256]{1,0:T(8,128)(2,1)S(1)}, bf16[512,256]{1,0:T(8,128)(2,1)}, u32[]{:S(2)}) copy-start(bf16[512,256]{1,0:T(8,128)(2,1)} %constant.19.clone.z_low) | copy-start | bytes 786436
  59.3 23.5 %copy-start.2 = (bf16[512,256]{1,0:T(8,128)(2,1)S(1)}, bf16[512,256]{1,0:T(8,128)(2,1)}, u32[]{:S(2)}) copy-start(bf16[512,256]{1,0:T(8,128)(2,1)} %constant.18.clone.z_high) | copy-start | bytes 786436

commit v4 on v3

--- a/solution.py
+++ b/solution.py
@@ -12,6 +12,7 @@
 N = 256
 ORIENT = 6
 IMG = 8
+WAIT = 4
 BF16 = jnp.bfloat16
 F32 = jnp.float32
 
@@ -62,10 +63,12 @@
 
 
 def front_kernel(
-    scalars, images_hbm, in_plane_hbm, tables,
+    scalars_in, images_hbm, in_plane_hbm, tables,
     keep, send,
-    total, images, in_plane, x_rows, big_sems, image_sems,
+    total, images, in_plane, x_rows, scalars, big_sems, image_sems,
 ):
+    scalar_copy = pltpu.make_async_copy(scalars_in, scalars, big_sems.at[2])
+    scalar_copy.start()
     image_copies = [
         pltpu.make_async_copy(images_hbm.at[p], images.at[p], image_sems.at[p]) for p in range(IMG)
     ]
@@ -74,6 +77,7 @@
     plane_copy = pltpu.make_async_copy(in_plane_hbm, in_plane, big_sems.at[0])
     table_copy = pltpu.make_async_copy(tables.at[0], x_rows, big_sems.at[1])
     total[...] = jnp.zeros_like(total)
+    scalar_copy.wait()
     position = lax.broadcasted_iota(jnp.int32, (IMG, N), 1)
     freq = jnp.where(position < N // 2, position, position - N).astype(F32)
     row = lax.broadcasted_iota(jnp.int32, (IMG, N), 0)
@@ -102,12 +106,14 @@
     sines = jnp.sin(angles)
     cosines = jnp.cos(angles)
     columns = jnp.concatenate([sines, cosines, jnp.zeros((64, N), F32)], axis=0).T
-    for copy in image_copies:
-        copy.wait()
-    plane_copy.start()
-    table_copy.start()
     chunk = 32
     for p in range(IMG):
+        if p % WAIT == 0:
+            for copy in image_copies[p : p + WAIT]:
+                copy.wait()
+        if p == 0:
+            plane_copy.start()
+            table_copy.start()
         sin_tx, sin_fx = sines[16 + p : 17 + p], sines[24 + p : 25 + p]
         cos_tx, cos_fx = cosines[16 + p : 17 + p], cosines[24 + p : 25 + p]
         which = classes[p]
@@ -137,9 +143,11 @@
         low_half, high_half = along[:, :128], along[:, 128:]
         own = jnp.where(first, low_half, high_half)
         other = jnp.where(first, high_half, low_half)
+        rows = slice(64 * (o % 3), 64 * (o % 3) + 64)
         for d in range(8):
-            keep[d, 64 * o : 64 * o + 64, :] = own[64 * d : 64 * d + 64]
-            send[d, 64 * o : 64 * o + 64, :] = other[64 * d : 64 * d + 64]
+            to = 8 * (d // 4) + 4 * (o // 3) + d % 4
+            keep[to, rows, :] = own[64 * d : 64 * d + 64]
+            send[to, rows, :] = other[64 * d : 64 * d + 64]
 
 
 def fetch_kernel(after, slab_hbm, slab_rows, sems):
@@ -196,7 +204,6 @@
 
 
 VMEM_SPEC = pl.BlockSpec(memory_space=pltpu.VMEM)
-SMEM_SPEC = pl.BlockSpec(memory_space=pltpu.SMEM)
 HBM_SPEC = pl.BlockSpec(memory_space=pltpu.HBM)
 FRONT_LIMIT = 53500 * 1024
 FETCH_LIMIT = 44000 * 1024
@@ -214,26 +221,29 @@
 
 def on_device(images, orient_ids, shift_ids, group_ids, translations, defocus, in_plane, slab_rows):
     tables = jnp.asarray(np.stack([x_table()[0], *y_table()]))
-    codes = orient_ids + 8 * shift_ids + 128 * group_ids
+    spread = ((0, 1), (16, 8))
     scalars = (
         jnp.pad(translations.T, ((0, 0), (0, 16)))
-        + jnp.pad(codes.astype(F32)[None], ((0, 1), (16, 8)))
+        + jnp.pad(orient_ids[None], spread).astype(F32)
+        + jnp.pad(shift_ids[None], spread).astype(F32) * 8.0
+        + jnp.pad(group_ids[None], spread).astype(F32) * 128.0
         + jnp.pad(defocus[None], ((0, 1), (24, 0)))
     )
     keep, send = pl.pallas_call(
         front_kernel,
         out_shape=[
-            jax.ShapeDtypeStruct((8, 384, 128), BF16),
-            jax.ShapeDtypeStruct((8, 384, 128), BF16),
+            jax.ShapeDtypeStruct((16, 192, 128), BF16),
+            jax.ShapeDtypeStruct((16, 192, 128), BF16),
         ],
-        in_specs=[SMEM_SPEC] + [HBM_SPEC] * 3,
+        in_specs=[HBM_SPEC] * 4,
         out_specs=[VMEM_SPEC] * 2,
         scratch_shapes=[
             pltpu.VMEM((ORIENT, N, 2 * N), F32),
             pltpu.VMEM((IMG, N, 2 * N), BF16),
             pltpu.VMEM((ORIENT, N, N), BF16),
             pltpu.VMEM((512, 512), BF16),
-            pltpu.SemaphoreType.DMA((2,)),
+            pltpu.SMEM((2, 32), F32),
+            pltpu.SemaphoreType.DMA((3,)),
             pltpu.SemaphoreType.DMA((IMG,)),
         ],
         compiler_params=pltpu.CompilerParams(vmem_limit_bytes=FRONT_LIMIT),
@@ -244,7 +254,7 @@
     other = lax.ppermute(send, "co", [(0, 1), (1, 0)])
     pair = (keep.astype(F32) + other.astype(F32)).astype(BF16)
     pieces = lax.all_to_all(
-        pair.reshape(16, 192, 128), DOM + ("xl",), split_axis=0, concat_axis=0, tiled=True
+        pair, ("xh", "xl", "yy"), split_axis=0, concat_axis=0, tiled=True
     )
     part = total_of(pieces)
     pieces = lax.all_to_all(

time: 84.1 us -> 82.1 us (0.976)
  blocking collectives: 60.1 us -> 58.7 us
  starting transfers between devices: 7.94 us -> 8.8 us
    pallas_call x1, Pallas kernels: 5.57 us -> 4.7 us  [on_device(): pl.pallas_call(front_kernel, out_shape=[jax.ShapeDtypeStruct((16, 192, 12...]
    ppermute x3, starting transfers between devices: 4.62 us -> 5.47 us  [swap(): return lax.ppermute(array, ('xl', 'co'), [(i, i ^ bits) for i in range(4)])]
    all_to_all x1, blocking collectives: 20.4 us -> 19.6 us  [on_device(): lax.all_to_all(jnp.broadcast_to(part[None], (8, 192, 128)), 'zz', split_a...]
where the time goes in v4:
time: 82.1 us; the launch traced here: 81.9 us
  blocking collectives  58.7 us (71%)
  Pallas kernels  11.1 us (14%)
  starting transfers between devices  8.8 us (11%)
  waiting for transfers between devices  1.92 us (2%)
  other arithmetic  1.2 us (1%)
    all_to_all x1, blocking collectives, on_device(): lax.all_to_all(sent.reshape(256, 4, 128), ALL, split_axis=0, concat_axis=...  21 us
    all_to_all x1, blocking collectives, on_device(): lax.all_to_all(jnp.broadcast_to(part[None], (8, 192, 128)), 'zz', split_a...  19.6 us
    all_to_all x1, blocking collectives, on_device(): lax.all_to_all(pair, ('xh', 'xl', 'yy'), split_axis=0, concat_axis=0, til...  18.1 us
    ppermute x3, starting transfers between devices, swap(): return lax.ppermute(array, ('xl', 'co'), [(i, i ^ bits) for i in range(4)])  5.47 us
    pallas_call x1, Pallas kernels, on_device(): pl.pallas_call(front_kernel, out_shape=[jax.ShapeDtypeStruct((16, 192, 12...  4.7 us
    ppermute x1, starting transfers between devices, on_device(): other = lax.ppermute(send, 'co', [(0, 1), (1, 0)])  3.33 us
    pallas_call x1, Pallas kernels, on_device(): pl.pallas_call(fetch_kernel, out_shape=jax.ShapeDtypeStruct(slab_rows.sha...  2.85 us
    pallas_call x1, Pallas kernels, on_device(): pl.pallas_call(insert_kernel, out_shape=jax.ShapeDtypeStruct((8, 128, 128...  2.45 us
  transfers between devices with their start and end apart: 4, of which 1 were waited for; matrix products, arithmetic and copies ran while one was open for 0% of the time, Pallas kernels for 3%

profile of v4, /device:TPU:1, one launch (start us, length us, event | category | flops | bytes accessed | tf_op | source)
XLA Modules:
  0.0 81.9 jit_solution(9567882230583873616)
XLA Ops:
  0.0 0.8 %pad_add_fusion.scalars_in = f32[2,32]{1,0:T(2,128)S(1)} fusion(f32[1,8]{1,0:T(1,128)} %bitcast.10, s32[1,8]{1,0:T(1,128)} %bitcast.11, s32[1,8]{1,0:T(1,128)} %bitcast.12, s32[1,8]{1,0:T(1,128)} %bitcast.13, f32[2,16]{1,0:T(2,128)} %bitcast.9), kind=kLoop, calls=%fused_computation.1 | loop fusion | flops 576 | bytes 512 | tf_op jit(solution)/shard_map/add | solution.py:226
  0.8 4.7 %front.1 = (bf16[16,192,128]{2,1,0:T(8,128)(2,1)S(1)}, bf16[16,192,128]{2,1,0:T(8,128)(2,1)S(1)}) custom-call(f32[2,32]{1,0:T(2,128)S(1)} %pad_add_fusion.scalars_in, bf16[8,256,512]{2,1,0:T(8,128)(2,1)} %images_hbm.1, bf16[6,256,256]{2,1,0:T(8,128)(2,1)} %in_plane_hbm.1, bf16[3,512,512]{2,1,0:T(8,128)(2,1)} %constant.18.clone.tables), custom_call_target="tpu_custom_call" | custom-call | tf_op jit(solution)/shard_map/front/pallas_call | solution.py:232
  5.5 3.3 %collective-permute-start = (bf16[16,192,128]{2,1,0:T(8,128)(2,1)S(1)}, bf16[16,192,128]{2,1,0:T(8,128)(2,1)S(1)}, u32[]{:S(2)}, u32[]{:S(2)}) collective-permute-start(bf16[16,192,128]{2,1,0:T(8,128)(2,1)S(1)} %get-tuple-element.8), channel_id=1, source_target_pairs={{0,1},{1,0},{2,3},{3,2},{4,5},{5,4},{6,7},{7,6},{8,9},{9,8},{10,11... | collective-permute-start | bytes 2359304 | tf_op jit(solution)/shard_map/ppermute | solution.py:254
  8.9 1.9 %collective-permute-done = bf16[16,192,128]{2,1,0:T(8,128)(2,1)S(1)} collective-permute-done((bf16[16,192,128]{2,1,0:T(8,128)(2,1)S(1)}, bf16[16,192,128]{2,1,0:T(8,128)(2,1)S(1)}, u32[]{:S(2)}, u32[]{:S(2)}) %collective-permute-start) | collective-permute-done | bytes 786464 | tf_op jit(solution)/shard_map/ppermute | solution.py:254
  10.8 0.2 add_convert_fusion
  11.0 18.1 %all_to_all.15 = bf16[16,192,128]{2,1,0:T(8,128)(2,1)S(1)} all-to-all(bf16[16,192,128]{2,1,0:T(8,128)(2,1)S(1)} %add_convert_fusion), channel_id=1, replica_groups=mesh['xh'=2,'yy'=4,'zz'=8,'xl'=2,'co'=2] {'xh','xl','yy'}, dimensions={0} | all-to-all | bytes 1572864 | tf_op jit(solution)/shard_map/all_to_all | solution.py:256
  29.1 0.1 reduce_sum.24
  29.2 0.1 broadcast_in_dim.22
  29.3 19.6 %all_to_all.16 = bf16[8,192,128]{2,1,0:T(8,128)(2,1)S(1)} all-to-all(bf16[8,192,128]{2,1,0:T(8,128)(2,1)S(1)} %broadcast_in_dim.22), channel_id=1, replica_groups=mesh['xh'=2,'yy'=4,'zz'=8,'xl'=2,'co'=2] {'zz'}, dimensions={0} | all-to-all | bytes 786432 | tf_op jit(solution)/shard_map/all_to_all | solution.py:260
  48.9 0.1 reduce_sum.25.after.own
  48.9 0.0 copy-start
  48.9 3.5 %collective-permute-start.3 = (bf16[192,128]{1,0:T(8,128)(2,1)S(1)}, bf16[192,128]{1,0:T(8,128)(2,1)S(1)}, u32[]{:S(2)}, u32[]{:S(2)}) collective-permute-start(bf16[192,128]{1,0:T(8,128)(2,1)S(1)} %reduce_sum.25.after.own), channel_id=1, source_target_pairs={{0,3},{1,2},{2,1},{3,0},{4,7},{5,6},{6,5},{7,4},{8,11},{9,10},{10,... | collective-permute-start | bytes 147464 | tf_op jit(solution)/shard_map/ppermute | solution.py:215
  52.5 1.9 %collective-permute-start.2 = (bf16[192,128]{1,0:T(8,128)(2,1)S(1)}, bf16[192,128]{1,0:T(8,128)(2,1)S(1)}, u32[]{:S(2)}, u32[]{:S(2)}) collective-permute-start(bf16[192,128]{1,0:T(8,128)(2,1)S(1)} %reduce_sum.25.after.own), channel_id=1, source_target_pairs={{0,2},{1,3},{2,0},{3,1},{4,6},{5,7},{6,4},{7,5},{8,10},{9,11},{10,... | collective-permute-start | bytes 147464 | tf_op jit(solution)/shard_map/ppermute | solution.py:215
  54.4 0.0 collective-permute-start.1
  54.4 2.9 %fetch.1.slab_rows = bf16[6,8,256,256]{3,2,1,0:T(8,128)(2,1)S(1)} custom-call(bf16[192,128]{1,0:T(8,128)(2,1)S(1)} %reduce_sum.25.after.own, bf16[6,8,256,256]{3,2,1,0:T(8,128)(2,1)} %slab_hbm.1), custom_call_target="tpu_custom_call" | custom-call | bytes 12000000 | tf_op jit(solution)/shard_map/fetch/pallas_call | solution.py:264
  57.3 0.0 copy-start.1
  57.3 0.0 copy-start.2
  57.3 0.0 collective-permute-done.3.corner
  57.3 0.0 collective-permute-done.2.beside
  57.3 0.0 collective-permute-done.1.across
  57.3 0.0 copy-done
  57.3 2.4 %insert.1 = bf16[8,128,128]{2,1,0:T(8,128)(2,1)S(1)} custom-call(bf16[192,128]{1,0:T(8,128)(2,1)S(1)} %reduce_sum.25.after.own, bf16[192,128]{1,0:T(8,128)(2,1)S(1)} %collective-permute-done.1.across, bf16[192,128]{1,0:T(8,128)(2,1)S(1)} %collective-permute-done.2.beside, bf16[192,128]{1,0:T(8,128)(2,1)S(1)} %collective-permute-done.3.corner, ...), custom_call_target="tpu_custom_call" | custom-call | tf_op jit(solution)/shard_map/insert/pallas_call | solution.py:274
  59.8 21.0 %all_to_all.17 = bf16[256,4,128]{2,1,0:T(4,128)(2,1)S(1)} all-to-all(bf16[256,4,128]{2,1,0:T(4,128)(2,1)S(1)} %bitcast.7), channel_id=1, replica_groups=mesh['xh'=2,'yy'=4,'zz'=8,'xl'=2,'co'=2] {'xh','yy','zz','xl','co'}, dimensions={0} | all-to-all | bytes 524288 | tf_op jit(solution)/shard_map/all_to_all | solution.py:286
  80.8 0.0 copy-done.1
  80.8 0.0 copy-done.2
  80.8 1.1 %last.1 = f32[8,32,256]{2,1,0:T(8,128)} custom-call(bf16[8,128,128]{2,1,0:T(8,128)(2,1)S(1)} %bitcast.8, bf16[512,256]{1,0:T(8,128)(2,1)S(1)} %copy-done.2, bf16[512,256]{1,0:T(8,128)(2,1)S(1)} %copy-done.1), custom_call_target="tpu_custom_call" | custom-call | tf_op jit(solution)/shard_map/last/pallas_call | solution.py:290
Async XLA Ops:
  5.5 5.2 %collective-permute-start = (bf16[16,192,128]{2,1,0:T(8,128)(2,1)S(1)}, bf16[16,192,128]{2,1,0:T(8,128)(2,1)S(1)}, u32[]{:S(2)}, u32[]{:S(2)}) collective-permute-start(bf16[16,192,128]{2,1,0:T(8,128)(2,1)S(1)} %get-tuple-element.8), channel_id=1, source_target_pairs={{0,1},{1,0},{2,3},{3,2},{4,5},{5,4},{6,7},{7,6},{8,9},{9,8},{10,11... | collective-permute-start | bytes 2359304 | tf_op jit(solution)/shard_map/ppermute | solution.py:254
  48.9 8.4 %copy-start = (bf16[3,512,512]{2,1,0:T(8,128)(2,1)S(1)}, bf16[3,512,512]{2,1,0:T(8,128)(2,1)}, u32[]{:S(2)}) copy-start(bf16[3,512,512]{2,1,0:T(8,128)(2,1)} %constant.18.clone.tables) | copy-start | bytes 4718596
  48.9 8.4 %collective-permute-start.3 = (bf16[192,128]{1,0:T(8,128)(2,1)S(1)}, bf16[192,128]{1,0:T(8,128)(2,1)S(1)}, u32[]{:S(2)}, u32[]{:S(2)}) collective-permute-start(bf16[192,128]{1,0:T(8,128)(2,1)S(1)} %reduce_sum.25.after.own), channel_id=1, source_target_pairs={{0,3},{1,2},{2,1},{3,0},{4,7},{5,6},{6,5},{7,4},{8,11},{9,10},{10,... | collective-permute-start | bytes 147464 | tf_op jit(solution)/shard_map/ppermute | solution.py:215
  52.5 4.8 %collective-permute-start.2 = (bf16[192,128]{1,0:T(8,128)(2,1)S(1)}, bf16[192,128]{1,0:T(8,128)(2,1)S(1)}, u32[]{:S(2)}, u32[]{:S(2)}) collective-permute-start(bf16[192,128]{1,0:T(8,128)(2,1)S(1)} %reduce_sum.25.after.own), channel_id=1, source_target_pairs={{0,2},{1,3},{2,0},{3,1},{4,6},{5,7},{6,4},{7,5},{8,10},{9,11},{10,... | collective-permute-start | bytes 147464 | tf_op jit(solution)/shard_map/ppermute | solution.py:215
  54.4 2.9 %collective-permute-start.1 = (bf16[192,128]{1,0:T(8,128)(2,1)S(1)}, bf16[192,128]{1,0:T(8,128)(2,1)S(1)}, u32[]{:S(2)}, u32[]{:S(2)}) collective-permute-start(bf16[192,128]{1,0:T(8,128)(2,1)S(1)} %reduce_sum.25.after.own), channel_id=1, source_target_pairs={{0,1},{1,0},{2,3},{3,2},{4,5},{5,4},{6,7},{7,6},{8,9},{9,8},{10,11... | collective-permute-start | bytes 147464 | tf_op jit(solution)/shard_map/ppermute | solution.py:215
  57.3 23.5 %copy-start.1 = (bf16[512,256]{1,0:T(8,128)(2,1)S(1)}, bf16[512,256]{1,0:T(8,128)(2,1)}, u32[]{:S(2)}) copy-start(bf16[512,256]{1,0:T(8,128)(2,1)} %constant.20.clone.z_low) | copy-start | bytes 786436
  57.3 23.5 %copy-start.2 = (bf16[512,256]{1,0:T(8,128)(2,1)S(1)}, bf16[512,256]{1,0:T(8,128)(2,1)}, u32[]{:S(2)}) copy-start(bf16[512,256]{1,0:T(8,128)(2,1)} %constant.19.clone.z_high) | copy-start | bytes 786436

commit v5 on v4

--- a/solution.py
+++ b/solution.py
@@ -33,7 +33,7 @@
 
 
 def x_table():
-    x_of = (8 * np.arange(32)[None, :] + np.arange(8)[:, None]).reshape(-1)
+    x_of = (8 * np.arange(31, -1, -1)[None, :] + np.arange(8)[:, None]).reshape(-1)
     cosine, sine = (t.reshape(8, 32, N) for t in phases(x_of, np.arange(N)))
     real_rows = np.concatenate([cosine, -sine], axis=2)
     imag_rows = np.concatenate([sine, cosine], axis=2)
@@ -48,7 +48,7 @@
 
 
 def z_table():
-    half, slab, part = np.meshgrid(np.arange(2), np.arange(32), np.arange(4), indexing="ij")
+    half, slab, part = np.meshgrid(np.arange(2), np.arange(31, -1, -1), np.arange(4), indexing="ij")
     kz_of = (8 * slab + 4 * half + part).reshape(-1)
     cosine, sine = (t.reshape(2, 128, N) for t in phases(kz_of, np.arange(N)))
     return split_table(np.stack([cosine, -sine], axis=1).reshape(512, N))
@@ -145,7 +145,7 @@
         other = jnp.where(first, high_half, low_half)
         rows = slice(64 * (o % 3), 64 * (o % 3) + 64)
         for d in range(8):
-            to = 8 * (d // 4) + 4 * (o // 3) + d % 4
+            to = 15 - (8 * (d // 4) + 4 * (o // 3) + d % 4)
             keep[to, rows, :] = own[64 * d : 64 * d + 64]
             send[to, rows, :] = other[64 * d : 64 * d + 64]
 
@@ -187,8 +187,8 @@
         late = result[128:, 128 * e : 128 * e + 128]
         even = jnp.where(lane < 64, early, pltpu.roll(late, 64, 1))
         odd = jnp.where(lane < 64, pltpu.roll(early, 64, 1), late)
-        out[2 * e] = even.astype(BF16)
-        out[2 * e + 1] = odd.astype(BF16)
+        out[7 - 2 * e] = even.astype(BF16)
+        out[6 - 2 * e] = odd.astype(BF16)
 
 
 def last_kernel(pencils, z_high, z_low, out):
@@ -200,7 +200,7 @@
     stacked = jnp.concatenate(rows, axis=0)
     result = plain_dot(stacked, z_high[...]) + plain_dot(stacked, z_low[...])
     for d in range(8):
-        out[d] = result[32 * d : 32 * d + 32] * scaling
+        out[7 - d] = result[32 * d : 32 * d + 32] * scaling
 
 
 VMEM_SPEC = pl.BlockSpec(memory_space=pltpu.VMEM)
@@ -213,6 +213,18 @@
 
 def swap(array, bits):
     return lax.ppermute(array, ("xl", "co"), [(i, i ^ bits) for i in range(4)])
+
+
+def exchange(array, axes):
+    count = array.shape[0]
+    return lax.all_to_all(
+        array,
+        axes,
+        split_axis=0,
+        concat_axis=0,
+        tiled=True,
+        axis_index_groups=[list(range(count - 1, -1, -1))],
+    )
 
 
 def total_of(pieces):
@@ -253,13 +265,9 @@
     )
     other = lax.ppermute(send, "co", [(0, 1), (1, 0)])
     pair = (keep.astype(F32) + other.astype(F32)).astype(BF16)
-    pieces = lax.all_to_all(
-        pair, ("xh", "xl", "yy"), split_axis=0, concat_axis=0, tiled=True
-    )
+    pieces = exchange(pair, ("xh", "xl", "yy"))
     part = total_of(pieces)
-    pieces = lax.all_to_all(
-        jnp.broadcast_to(part[None], (8, 192, 128)), "zz", split_axis=0, concat_axis=0, tiled=True
-    )
+    pieces = exchange(jnp.broadcast_to(part[None], (8, 192, 128)), "zz")
     own = total_of(pieces)
     fetched = pl.pallas_call(
         fetch_kernel,
@@ -283,9 +291,7 @@
         compiler_params=pltpu.CompilerParams(vmem_limit_bytes=INSERT_LIMIT),
         name="insert",
     )(own, swap(own, 1), swap(own, 2), swap(own, 3), fetched, tables)
-    pencils = lax.all_to_all(
-        sent.reshape(256, 4, 128), ALL, split_axis=0, concat_axis=0, tiled=True
-    )
+    pencils = exchange(sent.reshape(256, 4, 128), ALL)
     z_high, z_low = z_table()
     return pl.pallas_call(
         last_kernel,

time: 82.1 us -> 80.3 us (0.978)
  blocking collectives: 58.7 us -> 56.7 us
    all_to_all x3, blocking collectives: 58.7 us -> 56.7 us  [exchange(): lax.all_to_all(array, axes, split_axis=0, concat_axis=0, tiled=True, axis...]
  transfers between devices with their start and end apart: 4 -> 4, of which waited for: 1 -> 2; matrix products, arithmetic and copies ran while one was open for 0% -> 0% of each run, Pallas kernels for 3% -> 4%
where the time goes in v5:
time: 80.3 us; the launch traced here: 80.1 us
  blocking collectives  56.7 us (71%)
  Pallas kernels  11.1 us (14%)
  starting transfers between devices  9 us (11%)
  waiting for transfers between devices  2.01 us (3%)
  other arithmetic  1.2 us (1%)
    all_to_all x3, blocking collectives, exchange(): lax.all_to_all(array, axes, split_axis=0, concat_axis=0, tiled=True, axis...  56.7 us
    ppermute x3, starting transfers between devices, swap(): return lax.ppermute(array, ('xl', 'co'), [(i, i ^ bits) for i in range(4)])  5.67 us
    pallas_call x1, Pallas kernels, on_device(): pl.pallas_call(front_kernel, out_shape=[jax.ShapeDtypeStruct((16, 192, 12...  4.7 us
    ppermute x1, starting transfers between devices, on_device(): other = lax.ppermute(send, 'co', [(0, 1), (1, 0)])  3.33 us
    pallas_call x1, Pallas kernels, on_device(): pl.pallas_call(fetch_kernel, out_shape=jax.ShapeDtypeStruct(slab_rows.sha...  2.85 us
    pallas_call x1, Pallas kernels, on_device(): pl.pallas_call(insert_kernel, out_shape=jax.ShapeDtypeStruct((8, 128, 128...  2.44 us
    ppermute x1, waiting for transfers between devices, on_device(): other = lax.ppermute(send, 'co', [(0, 1), (1, 0)])  1.91 us
  transfers between devices with their start and end apart: 4, of which 2 were waited for; matrix products, arithmetic and copies ran while one was open for 0% of the time, Pallas kernels for 4%

profile of v5, /device:TPU:1, one launch (start us, length us, event | category | flops | bytes accessed | tf_op | source)
XLA Modules:
  0.0 80.1 jit_solution(15811868631848361377)
XLA Ops:
  0.0 0.8 %pad_add_fusion.scalars_in = f32[2,32]{1,0:T(2,128)S(1)} fusion(f32[1,8]{1,0:T(1,128)} %bitcast.10, s32[1,8]{1,0:T(1,128)} %bitcast.11, s32[1,8]{1,0:T(1,128)} %bitcast.12, s32[1,8]{1,0:T(1,128)} %bitcast.13, f32[2,16]{1,0:T(2,128)} %bitcast.9), kind=kLoop, calls=%fused_computation.1 | loop fusion | flops 576 | bytes 512 | tf_op jit(solution)/shard_map/add | solution.py:238
  0.8 4.7 %front.1 = (bf16[16,192,128]{2,1,0:T(8,128)(2,1)S(1)}, bf16[16,192,128]{2,1,0:T(8,128)(2,1)S(1)}) custom-call(f32[2,32]{1,0:T(2,128)S(1)} %pad_add_fusion.scalars_in, bf16[8,256,512]{2,1,0:T(8,128)(2,1)} %images_hbm.1, bf16[6,256,256]{2,1,0:T(8,128)(2,1)} %in_plane_hbm.1, bf16[3,512,512]{2,1,0:T(8,128)(2,1)} %constant.18.clone.tables), custom_call_target="tpu_custom_call" | custom-call | tf_op jit(solution)/shard_map/front/pallas_call | solution.py:244
  5.5 3.3 %collective-permute-start = (bf16[16,192,128]{2,1,0:T(8,128)(2,1)S(1)}, bf16[16,192,128]{2,1,0:T(8,128)(2,1)S(1)}, u32[]{:S(2)}, u32[]{:S(2)}) collective-permute-start(bf16[16,192,128]{2,1,0:T(8,128)(2,1)S(1)} %get-tuple-element.8), channel_id=1, source_target_pairs={{0,1},{1,0},{2,3},{3,2},{4,5},{5,4},{6,7},{7,6},{8,9},{9,8},{10,11... | collective-permute-start | bytes 2359304 | tf_op jit(solution)/shard_map/ppermute | solution.py:266
  8.9 1.9 %collective-permute-done = bf16[16,192,128]{2,1,0:T(8,128)(2,1)S(1)} collective-permute-done((bf16[16,192,128]{2,1,0:T(8,128)(2,1)S(1)}, bf16[16,192,128]{2,1,0:T(8,128)(2,1)S(1)}, u32[]{:S(2)}, u32[]{:S(2)}) %collective-permute-start) | collective-permute-done | bytes 786464 | tf_op jit(solution)/shard_map/ppermute | solution.py:266
  10.8 0.2 add_convert_fusion
  11.0 15.6 %all_to_all.15 = bf16[16,192,128]{2,1,0:T(8,128)(2,1)S(1)} all-to-all(bf16[16,192,128]{2,1,0:T(8,128)(2,1)S(1)} %add_convert_fusion), channel_id=1, replica_groups={{226,194,162,130,224,192,160,128,98,66,34,2,96,64,32,0},{227,195,163,13..., dimensions={0} | all-to-all | bytes 1572864 | tf_op jit(solution)/shard_map/all_to_all | solution.py:220
  26.6 0.1 reduce_sum.24
  26.7 0.1 broadcast_in_dim.22
  26.7 15.7 %all_to_all.16 = bf16[8,192,128]{2,1,0:T(8,128)(2,1)S(1)} all-to-all(bf16[8,192,128]{2,1,0:T(8,128)(2,1)S(1)} %broadcast_in_dim.22), channel_id=1, replica_groups={{28,24,20,16,12,8,4,0},{29,25,21,17,13,9,5,1},{30,26,22,18,14,10,6,2},{..., dimensions={0} | all-to-all | bytes 786432 | tf_op jit(solution)/shard_map/all_to_all | solution.py:220
  42.5 0.1 reduce_sum.25.after.own
  42.5 0.0 copy-start
  42.6 5.2 %collective-permute-start.3 = (bf16[192,128]{1,0:T(8,128)(2,1)S(1)}, bf16[192,128]{1,0:T(8,128)(2,1)S(1)}, u32[]{:S(2)}, u32[]{:S(2)}) collective-permute-start(bf16[192,128]{1,0:T(8,128)(2,1)S(1)} %reduce_sum.25.after.own), channel_id=1, source_target_pairs={{0,3},{1,2},{2,1},{3,0},{4,7},{5,6},{6,5},{7,4},{8,11},{9,10},{10,... | collective-permute-start | bytes 147464 | tf_op jit(solution)/shard_map/ppermute | solution.py:215
  47.7 0.5 collective-permute-start.2
  48.2 0.0 collective-permute-start.1
  48.2 2.9 %fetch.1.slab_rows = bf16[6,8,256,256]{3,2,1,0:T(8,128)(2,1)S(1)} custom-call(bf16[192,128]{1,0:T(8,128)(2,1)S(1)} %reduce_sum.25.after.own, bf16[6,8,256,256]{3,2,1,0:T(8,128)(2,1)} %slab_hbm.1), custom_call_target="tpu_custom_call" | custom-call | bytes 12000000 | tf_op jit(solution)/shard_map/fetch/pallas_call | solution.py:272
  51.1 0.0 copy-start.1
  51.1 0.0 copy-start.2
  51.1 0.0 collective-permute-done.3.corner
  51.1 0.1 collective-permute-done.2.beside
  51.2 0.0 collective-permute-done.1.across
  51.2 0.0 copy-done
  51.2 2.4 %insert.1 = bf16[8,128,128]{2,1,0:T(8,128)(2,1)S(1)} custom-call(bf16[192,128]{1,0:T(8,128)(2,1)S(1)} %reduce_sum.25.after.own, bf16[192,128]{1,0:T(8,128)(2,1)S(1)} %collective-permute-done.1.across, bf16[192,128]{1,0:T(8,128)(2,1)S(1)} %collective-permute-done.2.beside, bf16[192,128]{1,0:T(8,128)(2,1)S(1)} %collective-permute-done.3.corner, ...), custom_call_target="tpu_custom_call" | custom-call | tf_op jit(solution)/shard_map/insert/pallas_call | solution.py:282
  53.7 25.4 %all_to_all.17 = bf16[256,4,128]{2,1,0:T(4,128)(2,1)S(1)} all-to-all(bf16[256,4,128]{2,1,0:T(4,128)(2,1)S(1)} %bitcast.7), channel_id=1, replica_groups={{255,254,253,252,251,250,249,248,247,246,245,244,243,242,241,240,239,23..., dimensions={0} | all-to-all | bytes 524288 | tf_op jit(solution)/shard_map/all_to_all | solution.py:220
  79.0 0.0 copy-done.1
  79.0 0.0 copy-done.2
  79.0 1.1 %last.1 = f32[8,32,256]{2,1,0:T(8,128)} custom-call(bf16[8,128,128]{2,1,0:T(8,128)(2,1)S(1)} %bitcast.8, bf16[512,256]{1,0:T(8,128)(2,1)S(1)} %copy-done.2, bf16[512,256]{1,0:T(8,128)(2,1)S(1)} %copy-done.1), custom_call_target="tpu_custom_call" | custom-call | tf_op jit(solution)/shard_map/last/pallas_call | solution.py:296
Async XLA Ops:
  5.5 5.2 %collective-permute-start = (bf16[16,192,128]{2,1,0:T(8,128)(2,1)S(1)}, bf16[16,192,128]{2,1,0:T(8,128)(2,1)S(1)}, u32[]{:S(2)}, u32[]{:S(2)}) collective-permute-start(bf16[16,192,128]{2,1,0:T(8,128)(2,1)S(1)} %get-tuple-element.8), channel_id=1, source_target_pairs={{0,1},{1,0},{2,3},{3,2},{4,5},{5,4},{6,7},{7,6},{8,9},{9,8},{10,11... | collective-permute-start | bytes 2359304 | tf_op jit(solution)/shard_map/ppermute | solution.py:266
  42.5 8.7 %copy-start = (bf16[3,512,512]{2,1,0:T(8,128)(2,1)S(1)}, bf16[3,512,512]{2,1,0:T(8,128)(2,1)}, u32[]{:S(2)}) copy-start(bf16[3,512,512]{2,1,0:T(8,128)(2,1)} %constant.18.clone.tables) | copy-start | bytes 4718596
  42.6 8.6 %collective-permute-start.3 = (bf16[192,128]{1,0:T(8,128)(2,1)S(1)}, bf16[192,128]{1,0:T(8,128)(2,1)S(1)}, u32[]{:S(2)}, u32[]{:S(2)}) collective-permute-start(bf16[192,128]{1,0:T(8,128)(2,1)S(1)} %reduce_sum.25.after.own), channel_id=1, source_target_pairs={{0,3},{1,2},{2,1},{3,0},{4,7},{5,6},{6,5},{7,4},{8,11},{9,10},{10,... | collective-permute-start | bytes 147464 | tf_op jit(solution)/shard_map/ppermute | solution.py:215
  47.7 3.5 %collective-permute-start.2 = (bf16[192,128]{1,0:T(8,128)(2,1)S(1)}, bf16[192,128]{1,0:T(8,128)(2,1)S(1)}, u32[]{:S(2)}, u32[]{:S(2)}) collective-permute-start(bf16[192,128]{1,0:T(8,128)(2,1)S(1)} %reduce_sum.25.after.own), channel_id=1, source_target_pairs={{0,2},{1,3},{2,0},{3,1},{4,6},{5,7},{6,4},{7,5},{8,10},{9,11},{10,... | collective-permute-start | bytes 147464 | tf_op jit(solution)/shard_map/ppermute | solution.py:215
  48.2 3.0 %collective-permute-start.1 = (bf16[192,128]{1,0:T(8,128)(2,1)S(1)}, bf16[192,128]{1,0:T(8,128)(2,1)S(1)}, u32[]{:S(2)}, u32[]{:S(2)}) collective-permute-start(bf16[192,128]{1,0:T(8,128)(2,1)S(1)} %reduce_sum.25.after.own), channel_id=1, source_target_pairs={{0,1},{1,0},{2,3},{3,2},{4,5},{5,4},{6,7},{7,6},{8,9},{9,8},{10,11... | collective-permute-start | bytes 147464 | tf_op jit(solution)/shard_map/ppermute | solution.py:215
  51.1 28.0 %copy-start.1 = (bf16[512,256]{1,0:T(8,128)(2,1)S(1)}, bf16[512,256]{1,0:T(8,128)(2,1)}, u32[]{:S(2)}) copy-start(bf16[512,256]{1,0:T(8,128)(2,1)} %constant.20.clone.z_low) | copy-start | bytes 786436
  51.1 27.9 %copy-start.2 = (bf16[512,256]{1,0:T(8,128)(2,1)S(1)}, bf16[512,256]{1,0:T(8,128)(2,1)}, u32[]{:S(2)}) copy-start(bf16[512,256]{1,0:T(8,128)(2,1)} %constant.19.clone.z_high) | copy-start | bytes 786436

commit v6 on v5

--- a/solution.py
+++ b/solution.py
@@ -13,6 +13,7 @@
 ORIENT = 6
 IMG = 8
 WAIT = 4
+EARLY = 3
 BF16 = jnp.bfloat16
 F32 = jnp.float32
 
@@ -153,7 +154,7 @@
 def fetch_kernel(after, slab_hbm, slab_rows, sems):
     del after
     copies = [
-        pltpu.make_async_copy(slab_hbm.at[o], slab_rows.at[o], sems.at[o]) for o in range(ORIENT)
+        pltpu.make_async_copy(slab_hbm.at[o], slab_rows.at[o], sems.at[o]) for o in range(EARLY)
     ]
     for copy in copies:
         copy.start()
@@ -161,18 +162,38 @@
         copy.wait()
 
 
-def insert_kernel(own, across, beside, corner, slab_rows, tables, out, rows_all, spectrum):
+def insert_kernel(
+    own, across, beside, corner, early_rows, slab_hbm, tables, out,
+    rows_all, spectrum, partial, late_rows, sems,
+):
+    copies = [
+        pltpu.make_async_copy(slab_hbm.at[o], late_rows.at[o - EARLY], sems.at[o - EARLY])
+        for o in range(EARLY, ORIENT)
+    ]
+    for copy in copies:
+        copy.start()
     side, core = lax.axis_index("xl"), lax.axis_index("co")
     rows_all[side, core] = own[...]
     rows_all[side, 1 - core] = across[...]
     rows_all[1 - side, core] = beside[...]
     rows_all[1 - side, 1 - core] = corner[...]
+    factors = [
+        jnp.concatenate(
+            [rows_all[o // 3, c, 64 * (o % 3) : 64 * (o % 3) + 64, :] for c in range(2)], axis=1
+        )
+        for o in range(ORIENT)
+    ]
     for plane in range(8):
         found = jnp.zeros((64, N), F32)
-        for o in range(ORIENT):
-            rows = slice(64 * (o % 3), 64 * (o % 3) + 64)
-            factor = jnp.concatenate([rows_all[o // 3, c, rows, :] for c in range(2)], axis=1)
-            found += rows_dot(factor, slab_rows[o, plane])
+        for o in range(EARLY):
+            found += rows_dot(factors[o], early_rows[o, plane])
+        partial[plane] = found
+    for copy in copies:
+        copy.wait()
+    for plane in range(8):
+        found = partial[plane]
+        for o in range(EARLY, ORIENT):
+            found += rows_dot(factors[o], late_rows[o - EARLY, plane])
         start = (plane // 4) * 128 + plane % 4
         for part in range(4):
             rows, lanes = 32 * (part // 2), 128 * (part % 2)
@@ -206,8 +227,8 @@
 VMEM_SPEC = pl.BlockSpec(memory_space=pltpu.VMEM)
 HBM_SPEC = pl.BlockSpec(memory_space=pltpu.HBM)
 FRONT_LIMIT = 53500 * 1024
-FETCH_LIMIT = 44000 * 1024
-INSERT_LIMIT = 44000 * 1024
+FETCH_LIMIT = 49500 * 1024
+INSERT_LIMIT = 48000 * 1024
 LAST_LIMIT = 32768 * 1024
 
 
@@ -271,26 +292,29 @@
     own = total_of(pieces)
     fetched = pl.pallas_call(
         fetch_kernel,
-        out_shape=jax.ShapeDtypeStruct(slab_rows.shape, BF16),
+        out_shape=jax.ShapeDtypeStruct((EARLY, 8, N, N), BF16),
         in_specs=[VMEM_SPEC, HBM_SPEC],
         out_specs=VMEM_SPEC,
-        scratch_shapes=[pltpu.SemaphoreType.DMA((ORIENT,))],
+        scratch_shapes=[pltpu.SemaphoreType.DMA((EARLY,))],
         compiler_params=pltpu.CompilerParams(vmem_limit_bytes=FETCH_LIMIT),
-        cost_estimate=pl.CostEstimate(flops=0, bytes_accessed=12_000_000, transcendentals=0),
+        cost_estimate=pl.CostEstimate(flops=0, bytes_accessed=6_000_000, transcendentals=0),
         name="fetch",
     )(own, slab_rows)
     sent = pl.pallas_call(
         insert_kernel,
         out_shape=jax.ShapeDtypeStruct((8, 128, 128), BF16),
-        in_specs=[VMEM_SPEC] * 6,
+        in_specs=[VMEM_SPEC] * 5 + [HBM_SPEC, VMEM_SPEC],
         out_specs=VMEM_SPEC,
         scratch_shapes=[
             pltpu.VMEM((2, 2, 192, 128), BF16),
             pltpu.VMEM((4, N, 128), F32),
+            pltpu.VMEM((8, 64, N), F32),
+            pltpu.VMEM((ORIENT - EARLY, 8, N, N), BF16),
+            pltpu.SemaphoreType.DMA((ORIENT - EARLY,)),
         ],
         compiler_params=pltpu.CompilerParams(vmem_limit_bytes=INSERT_LIMIT),
         name="insert",
-    )(own, swap(own, 1), swap(own, 2), swap(own, 3), fetched, tables)
+    )(own, swap(own, 1), swap(own, 2), swap(own, 3), fetched, slab_rows, tables)
     pencils = exchange(sent.reshape(256, 4, 128), ALL)
     z_high, z_low = z_table()
     return pl.pallas_call(

time: 80.3 us -> 81.3 us (1.012)
  waiting for transfers between devices: 2.01 us -> 2.99 us
    pallas_call x1, Pallas kernels: 2.44 us -> 3.58 us  [on_device(): pl.pallas_call(insert_kernel, out_shape=jax.ShapeDtypeStruct((8, 128, 128...]
    ppermute x3, waiting for transfers between devices: 0.1 us -> 1.08 us  [swap(): return lax.ppermute(array, ('xl', 'co'), [(i, i ^ bits) for i in range(4)])]
    pallas_call x1, Pallas kernels: 2.85 us -> 1.88 us  [on_device(): pl.pallas_call(fetch_kernel, out_shape=jax.ShapeDtypeStruct((EARLY, 8, N,...]
  transfers between devices with their start and end apart: 4 -> 4, of which waited for: 2 -> 2; matrix products, arithmetic and copies ran while one was open for 0% -> 0% of each run, Pallas kernels for 4% -> 2%
where the time goes in v6:
time: 81.3 us; the launch traced here: 81 us
  blocking collectives  56.5 us (69%)
  Pallas kernels  11.2 us (14%)
  starting transfers between devices  9 us (11%)
  waiting for transfers between devices  2.99 us (4%)
  other arithmetic  1.2 us (1%)
    all_to_all x3, blocking collectives, exchange(): lax.all_to_all(array, axes, split_axis=0, concat_axis=0, tiled=True, axis...  56.5 us
    ppermute x3, starting transfers between devices, swap(): return lax.ppermute(array, ('xl', 'co'), [(i, i ^ bits) for i in range(4)])  5.67 us
    pallas_call x1, Pallas kernels, on_device(): pl.pallas_call(front_kernel, out_shape=[jax.ShapeDtypeStruct((16, 192, 12...  4.7 us
    pallas_call x1, Pallas kernels, on_device(): pl.pallas_call(insert_kernel, out_shape=jax.ShapeDtypeStruct((8, 128, 128...  3.58 us
    ppermute x1, starting transfers between devices, on_device(): other = lax.ppermute(send, 'co', [(0, 1), (1, 0)])  3.33 us
    ppermute x1, waiting for transfers between devices, on_device(): other = lax.ppermute(send, 'co', [(0, 1), (1, 0)])  1.91 us
    pallas_call x1, Pallas kernels, on_device(): pl.pallas_call(fetch_kernel, out_shape=jax.ShapeDtypeStruct((EARLY, 8, N,...  1.88 us
  transfers between devices with their start and end apart: 4, of which 2 were waited for; matrix products, arithmetic and copies ran while one was open for 0% of the time, Pallas kernels for 2%

profile of v6, /device:TPU:1, one launch (start us, length us, event | category | flops | bytes accessed | tf_op | source)
XLA Modules:
  0.0 81.0 jit_solution(17399508094231778146)
XLA Ops:
  0.0 0.8 %pad_add_fusion.scalars_in = f32[2,32]{1,0:T(2,128)S(1)} fusion(f32[1,8]{1,0:T(1,128)} %bitcast.10, s32[1,8]{1,0:T(1,128)} %bitcast.11, s32[1,8]{1,0:T(1,128)} %bitcast.12, s32[1,8]{1,0:T(1,128)} %bitcast.13, f32[2,16]{1,0:T(2,128)} %bitcast.9), kind=kLoop, calls=%fused_computation.1 | loop fusion | flops 576 | bytes 512 | tf_op jit(solution)/shard_map/add | solution.py:259
  0.8 4.7 %front.1 = (bf16[16,192,128]{2,1,0:T(8,128)(2,1)S(1)}, bf16[16,192,128]{2,1,0:T(8,128)(2,1)S(1)}) custom-call(f32[2,32]{1,0:T(2,128)S(1)} %pad_add_fusion.scalars_in, bf16[8,256,512]{2,1,0:T(8,128)(2,1)} %images_hbm.1, bf16[6,256,256]{2,1,0:T(8,128)(2,1)} %in_plane_hbm.1, bf16[3,512,512]{2,1,0:T(8,128)(2,1)} %constant.18.clone.tables), custom_call_target="tpu_custom_call" | custom-call | tf_op jit(solution)/shard_map/front/pallas_call | solution.py:265
  5.5 3.3 %collective-permute-start = (bf16[16,192,128]{2,1,0:T(8,128)(2,1)S(1)}, bf16[16,192,128]{2,1,0:T(8,128)(2,1)S(1)}, u32[]{:S(2)}, u32[]{:S(2)}) collective-permute-start(bf16[16,192,128]{2,1,0:T(8,128)(2,1)S(1)} %get-tuple-element.8), channel_id=1, source_target_pairs={{0,1},{1,0},{2,3},{3,2},{4,5},{5,4},{6,7},{7,6},{8,9},{9,8},{10,11... | collective-permute-start | bytes 2359304 | tf_op jit(solution)/shard_map/ppermute | solution.py:287
  8.9 1.9 %collective-permute-done = bf16[16,192,128]{2,1,0:T(8,128)(2,1)S(1)} collective-permute-done((bf16[16,192,128]{2,1,0:T(8,128)(2,1)S(1)}, bf16[16,192,128]{2,1,0:T(8,128)(2,1)S(1)}, u32[]{:S(2)}, u32[]{:S(2)}) %collective-permute-start) | collective-permute-done | bytes 786464 | tf_op jit(solution)/shard_map/ppermute | solution.py:287
  10.8 0.2 add_convert_fusion
  11.0 15.6 %all_to_all.15 = bf16[16,192,128]{2,1,0:T(8,128)(2,1)S(1)} all-to-all(bf16[16,192,128]{2,1,0:T(8,128)(2,1)S(1)} %add_convert_fusion), channel_id=1, replica_groups={{226,194,162,130,224,192,160,128,98,66,34,2,96,64,32,0},{227,195,163,13..., dimensions={0} | all-to-all | bytes 1572864 | tf_op jit(solution)/shard_map/all_to_all | solution.py:241
  26.6 0.1 reduce_sum.24
  26.7 0.1 broadcast_in_dim.22
  26.7 15.7 %all_to_all.16 = bf16[8,192,128]{2,1,0:T(8,128)(2,1)S(1)} all-to-all(bf16[8,192,128]{2,1,0:T(8,128)(2,1)S(1)} %broadcast_in_dim.22), channel_id=1, replica_groups={{28,24,20,16,12,8,4,0},{29,25,21,17,13,9,5,1},{30,26,22,18,14,10,6,2},{..., dimensions={0} | all-to-all | bytes 786432 | tf_op jit(solution)/shard_map/all_to_all | solution.py:241
  42.5 0.1 reduce_sum.25.after.own
  42.5 0.0 copy-start
  42.6 5.2 %collective-permute-start.3 = (bf16[192,128]{1,0:T(8,128)(2,1)S(1)}, bf16[192,128]{1,0:T(8,128)(2,1)S(1)}, u32[]{:S(2)}, u32[]{:S(2)}) collective-permute-start(bf16[192,128]{1,0:T(8,128)(2,1)S(1)} %reduce_sum.25.after.own), channel_id=1, source_target_pairs={{0,3},{1,2},{2,1},{3,0},{4,7},{5,6},{6,5},{7,4},{8,11},{9,10},{10,... | collective-permute-start | bytes 147464 | tf_op jit(solution)/shard_map/ppermute | solution.py:236
  47.7 0.5 collective-permute-start.2
  48.2 0.0 collective-permute-start.1
  48.2 1.9 %fetch.1.early_rows = bf16[3,8,256,256]{3,2,1,0:T(8,128)(2,1)S(1)} custom-call(bf16[192,128]{1,0:T(8,128)(2,1)S(1)} %reduce_sum.25.after.own, bf16[6,8,256,256]{3,2,1,0:T(8,128)(2,1)} %slab_hbm.3), custom_call_target="tpu_custom_call" | custom-call | bytes 6000000 | tf_op jit(solution)/shard_map/fetch/pallas_call | solution.py:293
  50.1 0.0 copy-start.1
  50.1 0.0 copy-start.2
  50.1 0.0 collective-permute-done.3.corner
  50.2 1.1 %collective-permute-done.2.beside = bf16[192,128]{1,0:T(8,128)(2,1)S(1)} collective-permute-done((bf16[192,128]{1,0:T(8,128)(2,1)S(1)}, bf16[192,128]{1,0:T(8,128)(2,1)S(1)}, u32[]{:S(2)}, u32[]{:S(2)}) %collective-permute-start.2) | collective-permute-done | bytes 49184 | tf_op jit(solution)/shard_map/ppermute | solution.py:236
  51.2 0.0 collective-permute-done.1.across
  51.2 0.0 copy-done
  51.2 3.6 %insert.1 = bf16[8,128,128]{2,1,0:T(8,128)(2,1)S(1)} custom-call(bf16[192,128]{1,0:T(8,128)(2,1)S(1)} %reduce_sum.25.after.own, bf16[192,128]{1,0:T(8,128)(2,1)S(1)} %collective-permute-done.1.across, bf16[192,128]{1,0:T(8,128)(2,1)S(1)} %collective-permute-done.2.beside, bf16[192,128]{1,0:T(8,128)(2,1)S(1)} %collective-permute-done.3.corner, ...), custom_call_target="tpu_custom_call" | custom-call | tf_op jit(solution)/shard_map/insert/pallas_call | solution.py:303
  54.8 25.1 %all_to_all.17 = bf16[256,4,128]{2,1,0:T(4,128)(2,1)S(1)} all-to-all(bf16[256,4,128]{2,1,0:T(4,128)(2,1)S(1)} %bitcast.7), channel_id=1, replica_groups={{255,254,253,252,251,250,249,248,247,246,245,244,243,242,241,240,239,23..., dimensions={0} | all-to-all | bytes 524288 | tf_op jit(solution)/shard_map/all_to_all | solution.py:241
  80.0 0.0 copy-done.1
  80.0 0.0 copy-done.2
  80.0 1.1 %last.1 = f32[8,32,256]{2,1,0:T(8,128)} custom-call(bf16[8,128,128]{2,1,0:T(8,128)(2,1)S(1)} %bitcast.8, bf16[512,256]{1,0:T(8,128)(2,1)S(1)} %copy-done.2, bf16[512,256]{1,0:T(8,128)(2,1)S(1)} %copy-done.1), custom_call_target="tpu_custom_call" | custom-call | tf_op jit(solution)/shard_map/last/pallas_call | solution.py:320
Async XLA Ops:
  5.5 5.2 %collective-permute-start = (bf16[16,192,128]{2,1,0:T(8,128)(2,1)S(1)}, bf16[16,192,128]{2,1,0:T(8,128)(2,1)S(1)}, u32[]{:S(2)}, u32[]{:S(2)}) collective-permute-start(bf16[16,192,128]{2,1,0:T(8,128)(2,1)S(1)} %get-tuple-element.8), channel_id=1, source_target_pairs={{0,1},{1,0},{2,3},{3,2},{4,5},{5,4},{6,7},{7,6},{8,9},{9,8},{10,11... | collective-permute-start | bytes 2359304 | tf_op jit(solution)/shard_map/ppermute | solution.py:287
  42.5 8.7 %copy-start = (bf16[3,512,512]{2,1,0:T(8,128)(2,1)S(1)}, bf16[3,512,512]{2,1,0:T(8,128)(2,1)}, u32[]{:S(2)}) copy-start(bf16[3,512,512]{2,1,0:T(8,128)(2,1)} %constant.18.clone.tables) | copy-start | bytes 4718596
  42.6 7.6 %collective-permute-start.3 = (bf16[192,128]{1,0:T(8,128)(2,1)S(1)}, bf16[192,128]{1,0:T(8,128)(2,1)S(1)}, u32[]{:S(2)}, u32[]{:S(2)}) collective-permute-start(bf16[192,128]{1,0:T(8,128)(2,1)S(1)} %reduce_sum.25.after.own), channel_id=1, source_target_pairs={{0,3},{1,2},{2,1},{3,0},{4,7},{5,6},{6,5},{7,4},{8,11},{9,10},{10,... | collective-permute-start | bytes 147464 | tf_op jit(solution)/shard_map/ppermute | solution.py:236
  47.7 3.5 %collective-permute-start.2 = (bf16[192,128]{1,0:T(8,128)(2,1)S(1)}, bf16[192,128]{1,0:T(8,128)(2,1)S(1)}, u32[]{:S(2)}, u32[]{:S(2)}) collective-permute-start(bf16[192,128]{1,0:T(8,128)(2,1)S(1)} %reduce_sum.25.after.own), channel_id=1, source_target_pairs={{0,2},{1,3},{2,0},{3,1},{4,6},{5,7},{6,4},{7,5},{8,10},{9,11},{10,... | collective-permute-start | bytes 147464 | tf_op jit(solution)/shard_map/ppermute | solution.py:236
  48.2 3.0 %collective-permute-start.1 = (bf16[192,128]{1,0:T(8,128)(2,1)S(1)}, bf16[192,128]{1,0:T(8,128)(2,1)S(1)}, u32[]{:S(2)}, u32[]{:S(2)}) collective-permute-start(bf16[192,128]{1,0:T(8,128)(2,1)S(1)} %reduce_sum.25.after.own), channel_id=1, source_target_pairs={{0,1},{1,0},{2,3},{3,2},{4,5},{5,4},{6,7},{7,6},{8,9},{9,8},{10,11... | collective-permute-start | bytes 147464 | tf_op jit(solution)/shard_map/ppermute | solution.py:236
  50.1 29.8 %copy-start.1 = (bf16[512,256]{1,0:T(8,128)(2,1)S(1)}, bf16[512,256]{1,0:T(8,128)(2,1)}, u32[]{:S(2)}) copy-start(bf16[512,256]{1,0:T(8,128)(2,1)} %constant.20.clone.z_low) | copy-start | bytes 786436
  50.1 29.8 %copy-start.2 = (bf16[512,256]{1,0:T(8,128)(2,1)S(1)}, bf16[512,256]{1,0:T(8,128)(2,1)}, u32[]{:S(2)}) copy-start(bf16[512,256]{1,0:T(8,128)(2,1)} %constant.19.clone.z_high) | copy-start | bytes 786436

commit v7 on v5

--- a/solution.py
+++ b/solution.py
@@ -1,3 +1,4 @@
+import functools
 import math
 
 import jax
@@ -13,6 +14,7 @@
 ORIENT = 6
 IMG = 8
 WAIT = 4
+EARLY = 2
 BF16 = jnp.bfloat16
 F32 = jnp.float32
 
@@ -150,10 +152,11 @@
             send[to, rows, :] = other[64 * d : 64 * d + 64]
 
 
-def fetch_kernel(after, slab_hbm, slab_rows, sems):
+def fetch_kernel(first, after, slab_hbm, slab_rows, sems):
     del after
     copies = [
-        pltpu.make_async_copy(slab_hbm.at[o], slab_rows.at[o], sems.at[o]) for o in range(ORIENT)
+        pltpu.make_async_copy(slab_hbm.at[first + i], slab_rows.at[i], sems.at[i])
+        for i in range(slab_rows.shape[0])
     ]
     for copy in copies:
         copy.start()
@@ -161,7 +164,7 @@
         copy.wait()
 
 
-def insert_kernel(own, across, beside, corner, slab_rows, tables, out, rows_all, spectrum):
+def insert_kernel(own, across, beside, corner, early, late, tables, out, rows_all, spectrum):
     side, core = lax.axis_index("xl"), lax.axis_index("co")
     rows_all[side, core] = own[...]
     rows_all[side, 1 - core] = across[...]
@@ -172,7 +175,7 @@
         for o in range(ORIENT):
             rows = slice(64 * (o % 3), 64 * (o % 3) + 64)
             factor = jnp.concatenate([rows_all[o // 3, c, rows, :] for c in range(2)], axis=1)
-            found += rows_dot(factor, slab_rows[o, plane])
+            found += rows_dot(factor, (early[o, plane] if o < EARLY else late[o - EARLY, plane]))
         start = (plane // 4) * 128 + plane % 4
         for part in range(4):
             rows, lanes = 32 * (part // 2), 128 * (part % 2)
@@ -206,7 +209,8 @@
 VMEM_SPEC = pl.BlockSpec(memory_space=pltpu.VMEM)
 HBM_SPEC = pl.BlockSpec(memory_space=pltpu.HBM)
 FRONT_LIMIT = 53500 * 1024
-FETCH_LIMIT = 44000 * 1024
+TOTAL_LIMIT = 8192 * 1024
+FETCH_LIMIT = 48500 * 1024
 INSERT_LIMIT = 44000 * 1024
 LAST_LIMIT = 32768 * 1024
 
@@ -225,6 +229,29 @@
         tiled=True,
         axis_index_groups=[list(range(count - 1, -1, -1))],
     )
+
+
+def fetch(first, count, after, slab_rows):
+    return pl.pallas_call(
+        functools.partial(fetch_kernel, first),
+        out_shape=jax.ShapeDtypeStruct((count, *slab_rows.shape[1:]), BF16),
+        in_specs=[VMEM_SPEC, HBM_SPEC],
+        out_specs=VMEM_SPEC,
+        scratch_shapes=[pltpu.SemaphoreType.DMA((count,))],
+        compiler_params=pltpu.CompilerParams(vmem_limit_bytes=FETCH_LIMIT),
+        cost_estimate=pl.CostEstimate(
+            flops=0, bytes_accessed=2_000_000 * count, transcendentals=0
+        ),
+        name="fetch",
+    )(after, slab_rows)
+
+
+def total_kernel(pieces, fetched, out):
+    del fetched
+    sums = pieces[0].astype(F32)
+    for i in range(1, pieces.shape[0]):
+        sums += pieces[i].astype(F32)
+    out[...] = sums.astype(BF16)
 
 
 def total_of(pieces):
@@ -267,22 +294,22 @@
     pair = (keep.astype(F32) + other.astype(F32)).astype(BF16)
     pieces = exchange(pair, ("xh", "xl", "yy"))
     part = total_of(pieces)
-    pieces = exchange(jnp.broadcast_to(part[None], (8, 192, 128)), "zz")
-    own = total_of(pieces)
-    fetched = pl.pallas_call(
-        fetch_kernel,
-        out_shape=jax.ShapeDtypeStruct(slab_rows.shape, BF16),
-        in_specs=[VMEM_SPEC, HBM_SPEC],
+    copies = jnp.broadcast_to(part[None], (8, 192, 128))
+    pieces = exchange(copies, "zz")
+    early = fetch(0, EARLY, copies, slab_rows)
+    own = pl.pallas_call(
+        total_kernel,
+        out_shape=jax.ShapeDtypeStruct((192, 128), BF16),
+        in_specs=[VMEM_SPEC, pl.BlockSpec(memory_space=pl.ANY)],
         out_specs=VMEM_SPEC,
-        scratch_shapes=[pltpu.SemaphoreType.DMA((ORIENT,))],
-        compiler_params=pltpu.CompilerParams(vmem_limit_bytes=FETCH_LIMIT),
-        cost_estimate=pl.CostEstimate(flops=0, bytes_accessed=12_000_000, transcendentals=0),
-        name="fetch",
-    )(own, slab_rows)
+        compiler_params=pltpu.CompilerParams(vmem_limit_bytes=TOTAL_LIMIT),
+        name="total",
+    )(pieces, early)
+    late = fetch(EARLY, ORIENT - EARLY, own, slab_rows)
     sent = pl.pallas_call(
         insert_kernel,
         out_shape=jax.ShapeDtypeStruct((8, 128, 128), BF16),
-        in_specs=[VMEM_SPEC] * 6,
+        in_specs=[VMEM_SPEC] * 7,
         out_specs=VMEM_SPEC,
         scratch_shapes=[
             pltpu.VMEM((2, 2, 192, 128), BF16),
@@ -290,7 +317,7 @@
         ],
         compiler_params=pltpu.CompilerParams(vmem_limit_bytes=INSERT_LIMIT),
         name="insert",
-    )(own, swap(own, 1), swap(own, 2), swap(own, 3), fetched, tables)
+    )(own, swap(own, 1), swap(own, 2), swap(own, 3), early, late, tables)
     pencils = exchange(sent.reshape(256, 4, 128), ALL)
     z_high, z_low = z_table()
     return pl.pallas_call(

time: 80.3 us -> 81.7 us (1.017)
  blocking collectives: 56.7 us -> 40.6 us
  starting transfers between devices: 9 us -> 18.6 us
  waiting for transfers between devices: 2.01 us -> 6.97 us
  Pallas kernels: 11.1 us -> 13.1 us
    all_to_all x3 -> x2, blocking collectives: 56.7 us -> 40.6 us  [exchange(): lax.all_to_all(array, axes, split_axis=0, concat_axis=0, tiled=True, axis...]
    all_to_all x0 -> x1, starting transfers between devices: none -> 8.97 us  [exchange(): lax.all_to_all(array, axes, split_axis=0, concat_axis=0, tiled=True, axis...]
    all_to_all x0 -> x1, waiting for transfers between devices: none -> 4.41 us  [exchange(): lax.all_to_all(array, axes, split_axis=0, concat_axis=0, tiled=True, axis...]
    pallas_call x1 -> x3, Pallas kernels: 2.85 us -> 4.85 us  [the longest x2 4.79 us: fetch(): pl.pallas_call(functools.partial(fetch_kernel, first), out_shape=jax.Shap...]
  transfers between devices with their start and end apart: 4 -> 5, of which waited for: 2 -> 3; matrix products, arithmetic and copies ran while one was open for 0% -> 0% of each run, Pallas kernels for 4% -> 6%
where the time goes in v7:
time: 81.7 us; the launch traced here: 81.3 us
  blocking collectives  40.6 us (50%)
  starting transfers between devices  18.6 us (23%)
  Pallas kernels  13.1 us (16%)
  waiting for transfers between devices  6.97 us (9%)
  other arithmetic  1.14 us (1%)
  local copies, waits for them, and re-layouts  0.82 us (1%)
    all_to_all x2, blocking collectives, exchange(): lax.all_to_all(array, axes, split_axis=0, concat_axis=0, tiled=True, axis...  40.6 us
    all_to_all x1, starting transfers between devices, exchange(): lax.all_to_all(array, axes, split_axis=0, concat_axis=0, tiled=True, axis...  8.97 us
    ppermute x3, starting transfers between devices, swap(): return lax.ppermute(array, ('xl', 'co'), [(i, i ^ bits) for i in range(4)])  6.32 us
    pallas_call x2, Pallas kernels, fetch(): pl.pallas_call(functools.partial(fetch_kernel, first), out_shape=jax.Shap...  4.79 us
    pallas_call x1, Pallas kernels, on_device(): pl.pallas_call(front_kernel, out_shape=[jax.ShapeDtypeStruct((16, 192, 12...  4.7 us
    all_to_all x1, waiting for transfers between devices, exchange(): lax.all_to_all(array, axes, split_axis=0, concat_axis=0, tiled=True, axis...  4.41 us
    ppermute x1, starting transfers between devices, on_device(): other = lax.ppermute(send, 'co', [(0, 1), (1, 0)])  3.33 us
    pallas_call x1, Pallas kernels, on_device(): pl.pallas_call(insert_kernel, out_shape=jax.ShapeDtypeStruct((8, 128, 128...  2.45 us
  transfers between devices with their start and end apart: 5, of which 3 were waited for; matrix products, arithmetic and copies ran while one was open for 0% of the time, Pallas kernels for 6%

profile of v7, /device:TPU:1, one launch (start us, length us, event | category | flops | bytes accessed | tf_op | source)
XLA Modules:
  0.0 81.3 jit_solution(17628382306931714226)
XLA Ops:
  0.0 0.8 %pad_add_fusion.scalars_in = f32[2,32]{1,0:T(2,128)S(1)} fusion(f32[1,8]{1,0:T(1,128)} %bitcast.10, s32[1,8]{1,0:T(1,128)} %bitcast.11, s32[1,8]{1,0:T(1,128)} %bitcast.12, s32[1,8]{1,0:T(1,128)} %bitcast.13, f32[2,16]{1,0:T(2,128)} %bitcast.9), kind=kLoop, calls=%fused_computation.1 | loop fusion | flops 576 | bytes 512 | tf_op jit(solution)/shard_map/add | solution.py:265
  0.8 4.7 %front.1 = (bf16[16,192,128]{2,1,0:T(8,128)(2,1)S(1)}, bf16[16,192,128]{2,1,0:T(8,128)(2,1)S(1)}) custom-call(f32[2,32]{1,0:T(2,128)S(1)} %pad_add_fusion.scalars_in, bf16[8,256,512]{2,1,0:T(8,128)(2,1)} %images_hbm.1, bf16[6,256,256]{2,1,0:T(8,128)(2,1)} %in_plane_hbm.1, bf16[3,512,512]{2,1,0:T(8,128)(2,1)} %constant.17.clone.tables), custom_call_target="tpu_custom_call" | custom-call | tf_op jit(solution)/shard_map/front/pallas_call | solution.py:271
  5.5 3.3 %collective-permute-start = (bf16[16,192,128]{2,1,0:T(8,128)(2,1)S(1)}, bf16[16,192,128]{2,1,0:T(8,128)(2,1)S(1)}, u32[]{:S(2)}, u32[]{:S(2)}) collective-permute-start(bf16[16,192,128]{2,1,0:T(8,128)(2,1)S(1)} %get-tuple-element.8), channel_id=1, source_target_pairs={{0,1},{1,0},{2,3},{3,2},{4,5},{5,4},{6,7},{7,6},{8,9},{9,8},{10,11... | collective-permute-start | bytes 2359304 | tf_op jit(solution)/shard_map/ppermute | solution.py:293
  8.9 1.9 %collective-permute-done = bf16[16,192,128]{2,1,0:T(8,128)(2,1)S(1)} collective-permute-done((bf16[16,192,128]{2,1,0:T(8,128)(2,1)S(1)}, bf16[16,192,128]{2,1,0:T(8,128)(2,1)S(1)}, u32[]{:S(2)}, u32[]{:S(2)}) %collective-permute-start) | collective-permute-done | bytes 786464 | tf_op jit(solution)/shard_map/ppermute | solution.py:293
  10.8 0.2 add_convert_fusion
  11.0 15.6 %all_to_all.15 = bf16[16,192,128]{2,1,0:T(8,128)(2,1)S(1)} all-to-all(bf16[16,192,128]{2,1,0:T(8,128)(2,1)S(1)} %add_convert_fusion), channel_id=1, replica_groups={{226,194,162,130,224,192,160,128,98,66,34,2,96,64,32,0},{227,195,163,13..., dimensions={0} | all-to-all | bytes 1572864 | tf_op jit(solution)/shard_map/all_to_all | solution.py:224
  26.6 0.1 reduce_sum.12
  26.7 0.8 broadcast_in_dim.22.after
  27.5 9.0 %all-to-all-start.1 = ((bf16[8,192,128]{2,1,0:T(8,128)(2,1)}), bf16[8,192,128]{2,1,0:T(8,128)(2,1)S(1)}, u32[]{:S(2)}, u32[]{:S(2)}) async-start(bf16[8,192,128]{2,1,0:T(8,128)(2,1)} %broadcast_in_dim.22.after), calls=%async_computation.1 | async-start | bytes 786432 | tf_op jit(solution)/shard_map/all_to_all | solution.py:224
  36.5 2.6 %fetch.2.fetched.early = bf16[2,8,256,256]{3,2,1,0:T(8,128)(2,1)S(1)} custom-call(bf16[8,192,128]{2,1,0:T(8,128)(2,1)} %broadcast_in_dim.22.after, bf16[6,8,256,256]{3,2,1,0:T(8,128)(2,1)} %slab_hbm.3), custom_call_target="tpu_custom_call" | custom-call | bytes 4000000 | tf_op jit(solution)/shard_map/fetch/pallas_call | solution.py:235
  39.0 4.4 %all-to-all-done.1.pieces = bf16[8,192,128]{2,1,0:T(8,128)(2,1)S(1)} async-done(((bf16[8,192,128]{2,1,0:T(8,128)(2,1)}), bf16[8,192,128]{2,1,0:T(8,128)(2,1)S(1)}, u32[]{:S(2)}, u32[]{:S(2)}) %all-to-all-start.1) | async-done | bytes 393248 | tf_op jit(solution)/shard_map/all_to_all | solution.py:224
  43.5 0.1 total.1.after.own
  43.5 0.0 copy-start
  43.5 5.6 %collective-permute-start.3 = (bf16[192,128]{1,0:T(8,128)(2,1)S(1)}, bf16[192,128]{1,0:T(8,128)(2,1)S(1)}, u32[]{:S(2)}, u32[]{:S(2)}) collective-permute-start(bf16[192,128]{1,0:T(8,128)(2,1)S(1)} %total.1.after.own), channel_id=1, source_target_pairs={{0,3},{1,2},{2,1},{3,0},{4,7},{5,6},{6,5},{7,4},{8,11},{9,10},{10,... | collective-permute-start | bytes 147464 | tf_op jit(solution)/shard_map/ppermute | solution.py:219
  49.1 0.7 collective-permute-start.2
  49.8 0.0 collective-permute-start.1
  49.9 2.2 %fetch.3.late = bf16[4,8,256,256]{3,2,1,0:T(8,128)(2,1)S(1)} custom-call(bf16[192,128]{1,0:T(8,128)(2,1)S(1)} %total.1.after.own, bf16[6,8,256,256]{3,2,1,0:T(8,128)(2,1)} %slab_hbm.3), custom_call_target="tpu_custom_call" | custom-call | bytes 8000000 | tf_op jit(solution)/shard_map/fetch/pallas_call | solution.py:235
  52.1 0.0 copy-start.1
  52.1 0.0 copy-start.2
  52.1 0.0 collective-permute-done.3.corner
  52.1 0.6 collective-permute-done.2.beside
  52.7 0.0 collective-permute-done.1.across
  52.7 0.0 copy-done
  52.7 2.4 %insert.1 = bf16[8,128,128]{2,1,0:T(8,128)(2,1)S(1)} custom-call(bf16[192,128]{1,0:T(8,128)(2,1)S(1)} %total.1.after.own, bf16[192,128]{1,0:T(8,128)(2,1)S(1)} %collective-permute-done.1.across, bf16[192,128]{1,0:T(8,128)(2,1)S(1)} %collective-permute-done.2.beside, bf16[192,128]{1,0:T(8,128)(2,1)S(1)} %collective-permute-done.3.corner, ...), custom_call_target="tpu_custom_call" | custom-call | tf_op jit(solution)/shard_map/insert/pallas_call | solution.py:309
  55.2 25.0 %all_to_all.16 = bf16[256,4,128]{2,1,0:T(4,128)(2,1)S(1)} all-to-all(bf16[256,4,128]{2,1,0:T(4,128)(2,1)S(1)} %bitcast.7), channel_id=1, replica_groups={{255,254,253,252,251,250,249,248,247,246,245,244,243,242,241,240,239,23..., dimensions={0} | all-to-all | bytes 524288 | tf_op jit(solution)/shard_map/all_to_all | solution.py:224
  80.3 0.0 copy-done.1
  80.3 0.0 copy-done.2
  80.3 1.1 %last.1 = f32[8,32,256]{2,1,0:T(8,128)} custom-call(bf16[8,128,128]{2,1,0:T(8,128)(2,1)S(1)} %bitcast.8, bf16[512,256]{1,0:T(8,128)(2,1)S(1)} %copy-done.2, bf16[512,256]{1,0:T(8,128)(2,1)S(1)} %copy-done.1), custom_call_target="tpu_custom_call" | custom-call | tf_op jit(solution)/shard_map/last/pallas_call | solution.py:323
Async XLA Ops:
  5.5 5.2 %collective-permute-start = (bf16[16,192,128]{2,1,0:T(8,128)(2,1)S(1)}, bf16[16,192,128]{2,1,0:T(8,128)(2,1)S(1)}, u32[]{:S(2)}, u32[]{:S(2)}) collective-permute-start(bf16[16,192,128]{2,1,0:T(8,128)(2,1)S(1)} %get-tuple-element.8), channel_id=1, source_target_pairs={{0,1},{1,0},{2,3},{3,2},{4,5},{5,4},{6,7},{7,6},{8,9},{9,8},{10,11... | collective-permute-start | bytes 2359304 | tf_op jit(solution)/shard_map/ppermute | solution.py:293
  27.5 16.0 %all-to-all-start.1 = ((bf16[8,192,128]{2,1,0:T(8,128)(2,1)}), bf16[8,192,128]{2,1,0:T(8,128)(2,1)S(1)}, u32[]{:S(2)}, u32[]{:S(2)}) async-start(bf16[8,192,128]{2,1,0:T(8,128)(2,1)} %broadcast_in_dim.22.after), calls=%async_computation.1 | async-start | bytes 786432 | tf_op jit(solution)/shard_map/all_to_all | solution.py:224
  43.5 9.2 %copy-start = (bf16[3,512,512]{2,1,0:T(8,128)(2,1)S(1)}, bf16[3,512,512]{2,1,0:T(8,128)(2,1)}, u32[]{:S(2)}) copy-start(bf16[3,512,512]{2,1,0:T(8,128)(2,1)} %constant.17.clone.tables) | copy-start | bytes 4718596
  43.5 8.6 %collective-permute-start.3 = (bf16[192,128]{1,0:T(8,128)(2,1)S(1)}, bf16[192,128]{1,0:T(8,128)(2,1)S(1)}, u32[]{:S(2)}, u32[]{:S(2)}) collective-permute-start(bf16[192,128]{1,0:T(8,128)(2,1)S(1)} %total.1.after.own), channel_id=1, source_target_pairs={{0,3},{1,2},{2,1},{3,0},{4,7},{5,6},{6,5},{7,4},{8,11},{9,10},{10,... | collective-permute-start | bytes 147464 | tf_op jit(solution)/shard_map/ppermute | solution.py:219
  49.1 3.6 %collective-permute-start.2 = (bf16[192,128]{1,0:T(8,128)(2,1)S(1)}, bf16[192,128]{1,0:T(8,128)(2,1)S(1)}, u32[]{:S(2)}, u32[]{:S(2)}) collective-permute-start(bf16[192,128]{1,0:T(8,128)(2,1)S(1)} %total.1.after.own), channel_id=1, source_target_pairs={{0,2},{1,3},{2,0},{3,1},{4,6},{5,7},{6,4},{7,5},{8,10},{9,11},{10,... | collective-permute-start | bytes 147464 | tf_op jit(solution)/shard_map/ppermute | solution.py:219
  49.8 2.9 %collective-permute-start.1 = (bf16[192,128]{1,0:T(8,128)(2,1)S(1)}, bf16[192,128]{1,0:T(8,128)(2,1)S(1)}, u32[]{:S(2)}, u32[]{:S(2)}) collective-permute-start(bf16[192,128]{1,0:T(8,128)(2,1)S(1)} %total.1.after.own), channel_id=1, source_target_pairs={{0,1},{1,0},{2,3},{3,2},{4,5},{5,4},{6,7},{7,6},{8,9},{9,8},{10,11... | collective-permute-start | bytes 147464 | tf_op jit(solution)/shard_map/ppermute | solution.py:219
  52.1 28.2 %copy-start.1 = (bf16[512,256]{1,0:T(8,128)(2,1)S(1)}, bf16[512,256]{1,0:T(8,128)(2,1)}, u32[]{:S(2)}) copy-start(bf16[512,256]{1,0:T(8,128)(2,1)} %constant.19.clone.z_low) | copy-start | bytes 786436
  52.1 28.2 %copy-start.2 = (bf16[512,256]{1,0:T(8,128)(2,1)S(1)}, bf16[512,256]{1,0:T(8,128)(2,1)}, u32[]{:S(2)}) copy-start(bf16[512,256]{1,0:T(8,128)(2,1)} %constant.18.clone.z_high) | copy-start | bytes 786436

commit v8 on v5

--- a/solution.py
+++ b/solution.py
@@ -153,7 +153,11 @@
 def fetch_kernel(after, slab_hbm, slab_rows, sems):
     del after
     copies = [
-        pltpu.make_async_copy(slab_hbm.at[o], slab_rows.at[o], sems.at[o]) for o in range(ORIENT)
+        pltpu.make_async_copy(
+            slab_hbm.at[o, pl.ds(4 * half, 4)], slab_rows.at[o, pl.ds(4 * half, 4)], sems.at[2 * o + half]
+        )
+        for o in range(ORIENT)
+        for half in range(2)
     ]
     for copy in copies:
         copy.start()
@@ -181,7 +185,7 @@
             ]
     lane = lax.broadcasted_iota(jnp.int32, (128, 128), 1)
     both = jnp.concatenate([spectrum[part] for part in range(4)], axis=1).astype(BF16)
-    result = plain_dot(both, tables[1]) + plain_dot(both, tables[2])
+    result = plain_dot(both, tables[0]) + plain_dot(both, tables[1])
     for e in range(4):
         early = result[:128, 128 * e : 128 * e + 128]
         late = result[128:, 128 * e : 128 * e + 128]
@@ -274,7 +278,7 @@
         out_shape=jax.ShapeDtypeStruct(slab_rows.shape, BF16),
         in_specs=[VMEM_SPEC, HBM_SPEC],
         out_specs=VMEM_SPEC,
-        scratch_shapes=[pltpu.SemaphoreType.DMA((ORIENT,))],
+        scratch_shapes=[pltpu.SemaphoreType.DMA((2 * ORIENT,))],
         compiler_params=pltpu.CompilerParams(vmem_limit_bytes=FETCH_LIMIT),
         cost_estimate=pl.CostEstimate(flops=0, bytes_accessed=12_000_000, transcendentals=0),
         name="fetch",
@@ -290,7 +294,7 @@
         ],
         compiler_params=pltpu.CompilerParams(vmem_limit_bytes=INSERT_LIMIT),
         name="insert",
-    )(own, swap(own, 1), swap(own, 2), swap(own, 3), fetched, tables)
+    )(own, swap(own, 1), swap(own, 2), swap(own, 3), fetched, jnp.asarray(np.stack(y_table())))
     pencils = exchange(sent.reshape(256, 4, 128), ALL)
     z_high, z_low = z_table()
     return pl.pallas_call(

time: 80.3 us -> 80.3 us (level)
  no operation moved by 1% of the time
where the time goes in v8:
time: 80.3 us; the launch traced here: 80.1 us
  blocking collectives  56.7 us (71%)
  Pallas kernels  11.1 us (14%)
  starting transfers between devices  9 us (11%)
  waiting for transfers between devices  1.99 us (2%)
  other arithmetic  1.2 us (1%)
    all_to_all x3, blocking collectives, exchange(): lax.all_to_all(array, axes, split_axis=0, concat_axis=0, tiled=True, axis...  56.7 us
    ppermute x3, starting transfers between devices, swap(): return lax.ppermute(array, ('xl', 'co'), [(i, i ^ bits) for i in range(4)])  5.67 us
    pallas_call x1, Pallas kernels, on_device(): pl.pallas_call(front_kernel, out_shape=[jax.ShapeDtypeStruct((16, 192, 12...  4.7 us
    ppermute x1, starting transfers between devices, on_device(): other = lax.ppermute(send, 'co', [(0, 1), (1, 0)])  3.33 us
    pallas_call x1, Pallas kernels, on_device(): pl.pallas_call(fetch_kernel, out_shape=jax.ShapeDtypeStruct(slab_rows.sha...  2.87 us
    pallas_call x1, Pallas kernels, on_device(): pl.pallas_call(insert_kernel, out_shape=jax.ShapeDtypeStruct((8, 128, 128...  2.44 us
    ppermute x1, waiting for transfers between devices, on_device(): other = lax.ppermute(send, 'co', [(0, 1), (1, 0)])  1.91 us
  transfers between devices with their start and end apart: 4, of which 2 were waited for; matrix products, arithmetic and copies ran while one was open for 0% of the time, Pallas kernels for 4%

profile of v8, /device:TPU:1, one launch (start us, length us, event | category | flops | bytes accessed | tf_op | source)
XLA Modules:
  0.0 80.1 jit_solution(11732931053248313110)
XLA Ops:
  0.0 0.8 %pad_add_fusion.scalars_in = f32[2,32]{1,0:T(2,128)S(1)} fusion(f32[1,8]{1,0:T(1,128)} %bitcast.10, s32[1,8]{1,0:T(1,128)} %bitcast.11, s32[1,8]{1,0:T(1,128)} %bitcast.12, s32[1,8]{1,0:T(1,128)} %bitcast.13, f32[2,16]{1,0:T(2,128)} %bitcast.9), kind=kLoop, calls=%fused_computation.1 | loop fusion | flops 576 | bytes 512 | tf_op jit(solution)/shard_map/add | solution.py:242
  0.8 4.7 %front.1 = (bf16[16,192,128]{2,1,0:T(8,128)(2,1)S(1)}, bf16[16,192,128]{2,1,0:T(8,128)(2,1)S(1)}) custom-call(f32[2,32]{1,0:T(2,128)S(1)} %pad_add_fusion.scalars_in, bf16[8,256,512]{2,1,0:T(8,128)(2,1)} %images_hbm.1, bf16[6,256,256]{2,1,0:T(8,128)(2,1)} %in_plane_hbm.1, bf16[3,512,512]{2,1,0:T(8,128)(2,1)} %constant.20.clone.tables), custom_call_target="tpu_custom_call" | custom-call | tf_op jit(solution)/shard_map/front/pallas_call | solution.py:248
  5.5 3.3 %collective-permute-start = (bf16[16,192,128]{2,1,0:T(8,128)(2,1)S(1)}, bf16[16,192,128]{2,1,0:T(8,128)(2,1)S(1)}, u32[]{:S(2)}, u32[]{:S(2)}) collective-permute-start(bf16[16,192,128]{2,1,0:T(8,128)(2,1)S(1)} %get-tuple-element.8), channel_id=1, source_target_pairs={{0,1},{1,0},{2,3},{3,2},{4,5},{5,4},{6,7},{7,6},{8,9},{9,8},{10,11... | collective-permute-start | bytes 2359304 | tf_op jit(solution)/shard_map/ppermute | solution.py:270
  8.9 1.9 %collective-permute-done = bf16[16,192,128]{2,1,0:T(8,128)(2,1)S(1)} collective-permute-done((bf16[16,192,128]{2,1,0:T(8,128)(2,1)S(1)}, bf16[16,192,128]{2,1,0:T(8,128)(2,1)S(1)}, u32[]{:S(2)}, u32[]{:S(2)}) %collective-permute-start) | collective-permute-done | bytes 786464 | tf_op jit(solution)/shard_map/ppermute | solution.py:270
  10.8 0.2 add_convert_fusion
  11.0 15.6 %all_to_all.15 = bf16[16,192,128]{2,1,0:T(8,128)(2,1)S(1)} all-to-all(bf16[16,192,128]{2,1,0:T(8,128)(2,1)S(1)} %add_convert_fusion), channel_id=1, replica_groups={{226,194,162,130,224,192,160,128,98,66,34,2,96,64,32,0},{227,195,163,13..., dimensions={0} | all-to-all | bytes 1572864 | tf_op jit(solution)/shard_map/all_to_all | solution.py:224
  26.6 0.1 reduce_sum.24
  26.7 0.1 broadcast_in_dim.22
  26.7 15.7 %all_to_all.16 = bf16[8,192,128]{2,1,0:T(8,128)(2,1)S(1)} all-to-all(bf16[8,192,128]{2,1,0:T(8,128)(2,1)S(1)} %broadcast_in_dim.22), channel_id=1, replica_groups={{28,24,20,16,12,8,4,0},{29,25,21,17,13,9,5,1},{30,26,22,18,14,10,6,2},{..., dimensions={0} | all-to-all | bytes 786432 | tf_op jit(solution)/shard_map/all_to_all | solution.py:224
  42.5 0.1 reduce_sum.25.after.own
  42.5 0.0 copy-start
  42.6 5.2 %collective-permute-start.3 = (bf16[192,128]{1,0:T(8,128)(2,1)S(1)}, bf16[192,128]{1,0:T(8,128)(2,1)S(1)}, u32[]{:S(2)}, u32[]{:S(2)}) collective-permute-start(bf16[192,128]{1,0:T(8,128)(2,1)S(1)} %reduce_sum.25.after.own), channel_id=1, source_target_pairs={{0,3},{1,2},{2,1},{3,0},{4,7},{5,6},{6,5},{7,4},{8,11},{9,10},{10,... | collective-permute-start | bytes 147464 | tf_op jit(solution)/shard_map/ppermute | solution.py:219
  47.7 0.5 collective-permute-start.2
  48.2 0.0 collective-permute-start.1
  48.2 2.9 %fetch.1.slab_rows = bf16[6,8,256,256]{3,2,1,0:T(8,128)(2,1)S(1)} custom-call(bf16[192,128]{1,0:T(8,128)(2,1)S(1)} %reduce_sum.25.after.own, bf16[6,8,256,256]{3,2,1,0:T(8,128)(2,1)} %slab_hbm.1), custom_call_target="tpu_custom_call" | custom-call | bytes 12000000 | tf_op jit(solution)/shard_map/fetch/pallas_call | solution.py:276
  51.1 0.0 copy-start.1
  51.1 0.0 copy-start.2
  51.1 0.0 collective-permute-done.3.corner
  51.1 0.1 collective-permute-done.2.beside
  51.2 0.0 collective-permute-done.1.across
  51.2 0.0 copy-done
  51.2 2.4 %insert.1 = bf16[8,128,128]{2,1,0:T(8,128)(2,1)S(1)} custom-call(bf16[192,128]{1,0:T(8,128)(2,1)S(1)} %reduce_sum.25.after.own, bf16[192,128]{1,0:T(8,128)(2,1)S(1)} %collective-permute-done.1.across, bf16[192,128]{1,0:T(8,128)(2,1)S(1)} %collective-permute-done.2.beside, bf16[192,128]{1,0:T(8,128)(2,1)S(1)} %collective-permute-done.3.corner, ...), custom_call_target="tpu_custom_call" | custom-call | tf_op jit(solution)/shard_map/insert/pallas_call | solution.py:286
  53.7 25.4 %all_to_all.17 = bf16[256,4,128]{2,1,0:T(4,128)(2,1)S(1)} all-to-all(bf16[256,4,128]{2,1,0:T(4,128)(2,1)S(1)} %bitcast.8), channel_id=1, replica_groups={{255,254,253,252,251,250,249,248,247,246,245,244,243,242,241,240,239,23..., dimensions={0} | all-to-all | bytes 524288 | tf_op jit(solution)/shard_map/all_to_all | solution.py:224
  79.1 0.0 copy-done.1
  79.1 0.0 copy-done.2
  79.1 1.1 %last.1 = f32[8,32,256]{2,1,0:T(8,128)} custom-call(bf16[8,128,128]{2,1,0:T(8,128)(2,1)S(1)} %bitcast.7, bf16[512,256]{1,0:T(8,128)(2,1)S(1)} %copy-done.2, bf16[512,256]{1,0:T(8,128)(2,1)S(1)} %copy-done.1), custom_call_target="tpu_custom_call" | custom-call | tf_op jit(solution)/shard_map/last/pallas_call | solution.py:300
Async XLA Ops:
  5.5 5.2 %collective-permute-start = (bf16[16,192,128]{2,1,0:T(8,128)(2,1)S(1)}, bf16[16,192,128]{2,1,0:T(8,128)(2,1)S(1)}, u32[]{:S(2)}, u32[]{:S(2)}) collective-permute-start(bf16[16,192,128]{2,1,0:T(8,128)(2,1)S(1)} %get-tuple-element.8), channel_id=1, source_target_pairs={{0,1},{1,0},{2,3},{3,2},{4,5},{5,4},{6,7},{7,6},{8,9},{9,8},{10,11... | collective-permute-start | bytes 2359304 | tf_op jit(solution)/shard_map/ppermute | solution.py:270
  42.5 8.7 %copy-start = (bf16[2,512,512]{2,1,0:T(8,128)(2,1)S(1)}, bf16[2,512,512]{2,1,0:T(8,128)(2,1)}, u32[]{:S(2)}) copy-start(bf16[2,512,512]{2,1,0:T(8,128)(2,1)} %constant.21.clone.tables) | copy-start | bytes 3145732
  42.6 8.6 %collective-permute-start.3 = (bf16[192,128]{1,0:T(8,128)(2,1)S(1)}, bf16[192,128]{1,0:T(8,128)(2,1)S(1)}, u32[]{:S(2)}, u32[]{:S(2)}) collective-permute-start(bf16[192,128]{1,0:T(8,128)(2,1)S(1)} %reduce_sum.25.after.own), channel_id=1, source_target_pairs={{0,3},{1,2},{2,1},{3,0},{4,7},{5,6},{6,5},{7,4},{8,11},{9,10},{10,... | collective-permute-start | bytes 147464 | tf_op jit(solution)/shard_map/ppermute | solution.py:219
  47.7 3.5 %collective-permute-start.2 = (bf16[192,128]{1,0:T(8,128)(2,1)S(1)}, bf16[192,128]{1,0:T(8,128)(2,1)S(1)}, u32[]{:S(2)}, u32[]{:S(2)}) collective-permute-start(bf16[192,128]{1,0:T(8,128)(2,1)S(1)} %reduce_sum.25.after.own), channel_id=1, source_target_pairs={{0,2},{1,3},{2,0},{3,1},{4,6},{5,7},{6,4},{7,5},{8,10},{9,11},{10,... | collective-permute-start | bytes 147464 | tf_op jit(solution)/shard_map/ppermute | solution.py:219
  48.2 3.0 %collective-permute-start.1 = (bf16[192,128]{1,0:T(8,128)(2,1)S(1)}, bf16[192,128]{1,0:T(8,128)(2,1)S(1)}, u32[]{:S(2)}, u32[]{:S(2)}) collective-permute-start(bf16[192,128]{1,0:T(8,128)(2,1)S(1)} %reduce_sum.25.after.own), channel_id=1, source_target_pairs={{0,1},{1,0},{2,3},{3,2},{4,5},{5,4},{6,7},{7,6},{8,9},{9,8},{10,11... | collective-permute-start | bytes 147464 | tf_op jit(solution)/shard_map/ppermute | solution.py:219
  51.1 28.0 %copy-start.1 = (bf16[512,256]{1,0:T(8,128)(2,1)S(1)}, bf16[512,256]{1,0:T(8,128)(2,1)}, u32[]{:S(2)}) copy-start(bf16[512,256]{1,0:T(8,128)(2,1)} %constant.23.clone.z_low) | copy-start | bytes 786436
  51.1 27.9 %copy-start.2 = (bf16[512,256]{1,0:T(8,128)(2,1)S(1)}, bf16[512,256]{1,0:T(8,128)(2,1)}, u32[]{:S(2)}) copy-start(bf16[512,256]{1,0:T(8,128)(2,1)} %constant.22.clone.z_high) | copy-start | bytes 786436
